TPU v7x, 32 devices: a whole 2x2x4 slice. The times are simulated.
32 devices in a mesh: grp: 4 (over z), row: 8 (over y, x, core).
Axes of the slice: x: 2, y: 2, z: 4, core: 2. Of those that a mesh axis runs over, the one named last changes fastest.
Arguments:
- design: bfloat16 [49152, 512], P(('grp', 'row')), may hold values from -0.29882812 to 0.29882812
- scales: bfloat16 [49152], P(('grp', 'row')), may hold values from 0.3984375 to 9.5
- buckets: int32 [49152], P(('grp', 'row')), may hold values from 0 to 1535
Outputs:
- sketch: float32 [6144, 512], P(('grp', 'row'))
- precond: float32 [512, 512], P('grp')
All inputs are finite; a program needn't handle non-finite values.
Results may differ from a plain program's by a relative error of at most 0.0003.
Values sent between devices are 32-bit elements; how exact they have to be, the bound alone decides.
A program may use at most 64 MiB of HBM per device.

v0:
```python
import jax
import jax.numpy as jnp
from jax import lax
from jax.sharding import PartitionSpec as P


def chol_upper(gram_matrix):
    return jnp.linalg.cholesky(gram_matrix).T


def self_gram(matrix):
    return lax.dot_general(
        matrix,
        matrix,
        (((0,), (0,)), ((), ())),
        precision=lax.Precision.HIGHEST,
        preferred_element_type=jnp.float32,
    )


def per_device(design, scales, buckets):
    row_count = design.shape[0]
    col_count = design.shape[1]
    row_parts = lax.axis_size("row")
    owned_rows = row_count // row_parts
    label_ids = lax.iota(jnp.int32, row_count)
    onehot_table = jnp.where(
        label_ids[:, None] == buckets[None, :], scales[None, :], jnp.zeros((), jnp.bfloat16)
    )
    partial_value = jnp.dot(onehot_table, design, preferred_element_type=jnp.float32).reshape(
        row_parts, owned_rows, col_count
    )
    arrived = lax.all_to_all(partial_value, "row", split_axis=0, concat_axis=0, tiled=True)
    sketch = jnp.sum(arrived, axis=0)
    local_gram = self_gram(sketch)
    whole_gram = lax.psum(local_gram, ("grp", "row"))
    factor = chol_upper(whole_gram)
    precond = factor / jnp.sqrt(jnp.float32(row_count * lax.axis_size("grp")))
    slab_rows = col_count // lax.axis_size("grp")
    slab_start = lax.axis_index("grp") * slab_rows
    precond_rows = lax.dynamic_slice_in_dim(precond, slab_start, slab_rows, 0)
    return (sketch, precond_rows)


def solution(mesh):
    in_specs = (P(("grp", "row"), None), P(("grp", "row")), P(("grp", "row")))
    out_specs = (P(("grp", "row"), None), P("grp", None))
    return jax.shard_map(
        per_device, mesh=mesh, in_specs=in_specs, out_specs=out_specs, check_vma=False
    )
```

profile of v0, /device:TPU:0, one launch (start us, length us, event | category | flops | bytes accessed | tf_op | source)
XLA Modules:
  0.0 288.1 jit_solution(8968136782259342151)
XLA Ops:
  7.2 1.4 copy-done
  8.6 3.3 %fusion.1 = f32[1536,512]{1,0:T(8,128)S(1)} fusion(bf16[1536,512]{1,0:T(8,128)(2,1)S(1)} %copy-done, s32[1536]{0:T(1024)} %param.5, bf16[1536]{0:T(1024)(128)(2,1)} %param.4), kind=kOutput, calls=%fused_computation.2 | convolution fusion | flops 2420637696 | bytes 4727808 | tf_op jit(solution)/shard_map/dot_general | solution.py:30
  11.9 42.9 %all_to_all.5 = f32[8,192,512]{2,1,0:T(8,128)} all-to-all(f32[8,192,512]{2,1,0:T(8,128)S(1)} %bitcast.28), channel_id=1, replica_groups=mesh['grp'=4,'row'=8] {'row'}, dimensions={0} | all-to-all | bytes 6291456 | tf_op jit(solution)/shard_map/all_to_all | solution.py:33
  54.8 2.3 reduce_sum.9
  57.1 2.1 fusion.22
  59.3 129.4 %all-reduce.3.cloned.1.call-done = f32[512,512]{0,1:T(8,128)} async-done(((f32[512,512]{0,1:T(8,128)}), f32[512,512]{0,1:T(8,128)}) %all-reduce.3.cloned.1.call-update) | async-done | bytes 1048592 | tf_op jit(solution)/shard_map/psum | solution.py:36
  188.6 1.6 copy.6
  190.2 2.5 fusion.6
  192.7 0.8 cholesky.266
  193.5 11.7 %cholesky.104 = f32[128,128]{1,0:T(8,128)S(1)} custom-call(f32[128,128]{1,0:T(8,128)S(1)} %cholesky.266), custom_call_target="Cholesky" | custom-call | tf_op jit(solution)/shard_map/jit(cholesky)/cholesky | solution.py:8
  205.4 9.8 %custom-call.27 = f32[1,128,128]{1,2,0:T(8,128)S(1)} custom-call(f32[1,128,128]{2,1,0:T(8,128)S(1)} %get-tuple-element.13), custom_call_target="InvertDiagBlocksLowerTriangular" | custom-call | tf_op jit(solution)/shard_map/jit(cholesky)/cholesky | solution.py:8
  215.2 1.2 constant_dynamic-update-slice_fusion.3
  216.5 1.3 convolution_subtract_fusion
  217.7 11.9 %cholesky.217 = f32[128,128]{1,0:T(8,128)S(1)} custom-call(f32[128,128]{1,0:T(8,128)S(1)} %cholesky.270), custom_call_target="Cholesky" | custom-call | tf_op jit(solution)/shard_map/jit(cholesky)/cholesky | solution.py:8
  229.6 9.8 %custom-call.28 = f32[1,128,128]{1,2,0:T(8,128)S(1)} custom-call(f32[1,128,128]{2,1,0:T(8,128)S(1)} %get-tuple-element.10), custom_call_target="InvertDiagBlocksLowerTriangular" | custom-call | tf_op jit(solution)/shard_map/jit(cholesky)/cholesky | solution.py:8
  239.7 1.3 convolution_subtract_fusion.1
  241.0 11.7 %cholesky.238 = f32[128,128]{1,0:T(8,128)S(1)} custom-call(f32[128,128]{1,0:T(8,128)S(1)} %cholesky.275), custom_call_target="Cholesky" | custom-call | tf_op jit(solution)/shard_map/jit(cholesky)/cholesky | solution.py:8
  252.8 0.7 compare_reduce_fusion.1
  253.5 9.8 %custom-call.29 = f32[1,128,128]{1,2,0:T(8,128)S(1)} custom-call(f32[1,128,128]{2,1,0:T(8,128)S(1)} %get-tuple-element.7), custom_call_target="InvertDiagBlocksLowerTriangular" | custom-call | tf_op jit(solution)/shard_map/jit(cholesky)/cholesky | solution.py:8
  263.5 1.2 convolution_subtract_fusion.2
  264.7 11.7 %cholesky.255 = f32[128,128]{1,0:T(8,128)S(1)} custom-call(f32[128,128]{1,0:T(8,128)S(1)} %convolution_subtract_fusion.2), custom_call_target="Cholesky" | custom-call | tf_op jit(solution)/shard_map/jit(cholesky)/cholesky | solution.py:8
  276.5 0.6 compare_reduce_fusion
  277.1 0.7 compare_reduce_fusion.2
  280.4 0.8 copy.7
  (15 shorter events, 0.9 us)
Async XLA Ops:
  7.2 1.4 copy-start
  7.2 181.5 %all-reduce.3.cloned.1.call-start = ((), (), s32[]{:S(2)}) async-start(), calls=%async_computation.1 | async-start | bytes 2097152 | tf_op jit(solution)/shard_map/psum | solution.py:36
  57.1 135.6 %copy-start.1 = (f32[192,512]{1,0:T(8,128)}, f32[192,512]{1,0:T(8,128)S(1)}, u32[]{:S(2)}) copy-start(f32[192,512]{1,0:T(8,128)S(1)} %reduce_sum.9) | copy-start | bytes 1179652
Sparse Core Ops, SparseCore 0:
  59.4 129.2 all-reduce.2
where the time goes:
time: 289 us; the launch traced here: 288 us
  waiting for transfers between devices  129 us (45%)
  other arithmetic  83.4 us (29%)
  blocking collectives  42.9 us (15%)
  between operations  16.7 us (6%)
  matrix products  10.9 us (4%)
  local copies, waits for them, and re-layouts  4.74 us (2%)
    psum x1, waiting for transfers between devices, per_device(): whole_gram = lax.psum(local_gram, ('grp', 'row'))  129 us
    another operation x14, other arithmetic, chol_upper(): return jnp.linalg.cholesky(gram_matrix).T  78.6 us
    all_to_all x1, blocking collectives, per_device(): lax.all_to_all(partial_value, 'row', split_axis=0, concat_axis=0, tiled=T...  42.9 us
  transfers between devices with their start and end apart: 1, of which 1 were waited for; matrix products, arithmetic and copies ran while one was open for 0% of the time, Pallas kernels for 0%

commit v1 on v0

v1 whole, which is shorter than its diff:
```python
import functools
import math

import jax
import jax.numpy as jnp
from jax import lax
from jax.experimental import pallas as pl
from jax.experimental.pallas import tpu as pltpu
from jax.sharding import PartitionSpec as P

MESH = pl.DeviceIdType.MESH
F32 = jnp.float32
BF16 = jnp.bfloat16
LANES = 128
PANEL = 16


def split3(value):
    high = value.astype(BF16)
    rest = value - high.astype(F32)
    mid = rest.astype(BF16)
    low = (rest - mid.astype(F32)).astype(BF16)
    return high, mid, low


def panel_factor(panel, offset):
    size, width = panel.shape
    tiles = width // LANES
    sub = lax.broadcasted_iota(jnp.int32, (size, LANES), 0)
    cols = [
        jnp.broadcast_to(panel[:, offset + k : offset + k + 1], (size, LANES))
        for k in range(size)
    ]
    parts = [panel[:, t * LANES : (t + 1) * LANES] for t in range(tiles)]
    scale = jnp.zeros((size, LANES), F32)
    for j in range(size):
        inv = lax.rsqrt(cols[j][j : j + 1, :])
        mult = cols[j] * inv
        scale = jnp.where(sub == j, inv, scale)
        for k in range(j + 1, size):
            cols[k] = cols[k] - mult * (cols[k][j : j + 1, :] * inv)
        below = jnp.where(sub > j, mult, 0.0)
        parts = [part - below * (part[j : j + 1, :] * inv) for part in parts]
    return [part * scale for part in parts]


def factor_kernel(scale, grp_ref, gram_ref, out_ref, work):
    size = work.shape[0]
    half = size // 2
    quarter = size // 4
    for h in range(2):
        cs = slice(h * half, (h + 1) * half)
        work[0:quarter, cs] = gram_ref[h, 0:quarter, :]
    work[quarter : 2 * quarter, quarter:half] = gram_ref[0, quarter : 2 * quarter, quarter:half]
    work[quarter : 2 * quarter, half:size] = gram_ref[1, quarter : 2 * quarter, :]
    work[3 * quarter : size, 3 * quarter : size] = gram_ref[0, quarter : 2 * quarter, 0:quarter]
    work[half : half + quarter // 2, half:size] = gram_ref[0, half : half + quarter // 2, :]
    work[half + quarter // 2 : 3 * quarter, half:size] = gram_ref[1, half : half + quarter // 2, :]
    factor_in_place(work)
    write_rows(scale, grp_ref, out_ref, work)


def factor_whole_kernel(scale, grp_ref, gram_ref, out_ref, work):
    work[...] = gram_ref[...]
    factor_in_place(work)
    write_rows(scale, grp_ref, out_ref, work)


def factor_in_place(work):
    size = work.shape[0]
    for base in range(0, size, LANES):
        for start in range(0, LANES, PANEL):
            row = base + start
            rows = panel_factor(work[row : row + PANEL, base:size], start)
            for t, part in enumerate(rows):
                work[row : row + PANEL, base + t * LANES : base + (t + 1) * LANES] = part
            if start + PANEL == LANES:
                break
            splits = [split3(part) for part in rows]
            h, m, l = splits[0]
            lhs = jnp.concatenate([h, h, m, h, l, m], axis=0)
            for t, (h, m, l) in enumerate(splits):
                rhs = jnp.concatenate([h, m, h, l, h, m], axis=0)
                prod = lax.dot_general(
                    lhs, rhs, (((0,), (0,)), ((), ())), preferred_element_type=F32
                )
                cs = slice(base + t * LANES, base + (t + 1) * LANES)
                work[row + PANEL : base + LANES, cs] = (
                    work[row + PANEL : base + LANES, cs] - prod[start + PANEL :, :]
                )
        rest = base + LANES
        for left in range(rest, size, LANES):
            lhs = work[base:rest, left : left + LANES]
            work[left : left + LANES, left:size] = work[left : left + LANES, left:size] - lax.dot_general(
                lhs,
                work[base:rest, left:size],
                (((0,), (0,)), ((), ())),
                precision=lax.Precision.HIGHEST,
                preferred_element_type=F32,
            )


def write_rows(scale, grp_ref, out_ref, work):
    size = work.shape[0]
    count = out_ref.shape[0]
    first = pl.multiple_of(grp_ref[0] * count, count)
    rows = first + lax.broadcasted_iota(jnp.int32, (count, size), 0)
    cols = lax.broadcasted_iota(jnp.int32, (count, size), 1)
    value = work[pl.ds(first, count), :] * scale
    out_ref[...] = jnp.where(cols >= rows, value, 0.0)


def factor_call(kernel, gram, size, slab_rows, scale):
    grp = lax.axis_index("grp").astype(jnp.int32).reshape((1,))

    return pl.pallas_call(
        functools.partial(kernel, scale),
        out_shape=jax.ShapeDtypeStruct((slab_rows, size), F32),
        in_specs=[
            pl.BlockSpec(memory_space=pltpu.SMEM),
            pl.BlockSpec(memory_space=pltpu.VMEM),
        ],
        out_specs=pl.BlockSpec(memory_space=pltpu.VMEM),
        scratch_shapes=[pltpu.VMEM((size, size), F32)],
        compiler_params=pltpu.CompilerParams(vmem_limit_bytes=32 * 1024 * 1024),
        name="factor",
    )(grp, gram)


def self_gram(matrix):
    return lax.dot_general(
        matrix,
        matrix,
        (((0,), (0,)), ((), ())),
        precision=lax.Precision.HIGHEST,
        preferred_element_type=F32,
    )


def per_device_general(design, scales, buckets):
    row_count = design.shape[0]
    col_count = design.shape[1]
    row_parts = lax.axis_size("row")
    owned_rows = row_count // row_parts
    label_ids = lax.iota(jnp.int32, row_count)
    onehot_table = jnp.where(
        label_ids[:, None] == buckets[None, :], scales[None, :], jnp.zeros((), BF16)
    )
    partial_value = jnp.dot(onehot_table, design, preferred_element_type=F32).reshape(
        row_parts, owned_rows, col_count
    )
    arrived = lax.all_to_all(partial_value, "row", split_axis=0, concat_axis=0, tiled=True)
    sketch = jnp.sum(arrived, axis=0)
    whole_gram = lax.psum(self_gram(sketch), ("grp", "row"))
    grp_count = lax.axis_size("grp")
    scale = 1.0 / math.sqrt(row_count * grp_count)
    slab = factor_call(factor_whole_kernel, whole_gram, col_count, col_count // grp_count, scale)
    return (sketch, slab)


def embed_kernel(
    design_ref, scales_ref, buckets_ref, sketch_ref, gram_ref,
    give, took, acc, near, gsum, gcore, gown, gnear, gz, gall,
    give_s, give_r, near_s, near_r, gcore_s, gcore_r, gnear_s, gnear_r, gz_s, gz_r,
    gback_s, gback_r, gpair_s, gpair_r,
):
    z = lax.axis_index("grp")
    row = lax.axis_index("row")
    c = lax.rem(row, 2)
    x = lax.rem(row // 2, 2)
    y = row // 4
    core_id = (z, row + 1 - 2 * c)
    x_id = (z, row + 2 - 4 * x)
    y_id = (z, row + 4 - 8 * y)
    z_near_id = (z + 1 - 2 * lax.rem(z, 2), row)
    z_far_id = (z + 2 - 4 * (z // 2), row)
    peers = (core_id, x_id, y_id, z_near_id, z_far_id)

    barrier = pltpu.get_barrier_semaphore()
    for peer in peers:
        pl.semaphore_signal(barrier, inc=1, device_id=peer, device_id_type=MESH)
    pl.semaphore_wait(barrier, len(peers))

    pending = []

    def send(src, dst, send_sem, recv_sem, peer):
        copy = pltpu.make_async_remote_copy(
            src_ref=src, dst_ref=dst, send_sem=send_sem, recv_sem=recv_sem,
            device_id=peer, device_id_type=MESH,
        )
        copy.start()
        pending.append(copy)
        return copy

    rows_all = design_ref.shape[0]
    owned = sketch_ref.shape[0]
    half = design_ref.shape[1] // 2

    def part(slot, core):
        ty = y if slot < 2 else 1 - y
        tx = x if slot % 2 == 0 else 1 - x
        base = (ty * 4 + tx * 2 + core) * owned
        labels = base + lax.broadcasted_iota(jnp.int32, (owned, rows_all), 0)
        table = jnp.where(labels == buckets_ref[...], scales_ref[...], 0.0).astype(BF16)
        return jnp.dot(table, design_ref[...], preferred_element_type=F32)

    order = (3, 2, 1, 0)
    from_core = {}
    for s in order:
        value = part(s, 1 - c)
        give[s, 0] = value[:, :half]
        give[s, 1] = value[:, half:]
        from_core[s] = send(give.at[s], took.at[s], give_s.at[s], give_r.at[s], core_id)
    for s in order:
        value = part(s, c)
        acc[s, 0] = value[:, :half]
        acc[s, 1] = value[:, half:]

    first = (x_id, y_id)
    second = (y_id, x_id)
    passed = (2, 1)
    direct = (1, 2)

    def near_send(slot, h, step):
        peer = second[h] if step == 2 else first[h]
        return send(acc.at[slot, h], near.at[h, step], near_s.at[h, step], near_r.at[h, step], peer)

    steps = {}
    for s in order:
        from_core[s].wait_recv()
        for h in range(2):
            acc[s, h] = acc[s, h] + took[s, h]
            if s == 3:
                steps[h, 0] = near_send(3, h, 0)
            elif s == direct[h]:
                steps[h, 1] = near_send(s, h, 1)
    for h in range(2):
        steps[h, 0].wait_recv()
        acc[passed[h], h] = acc[passed[h], h] + near[h, 0]
        steps[h, 2] = near_send(passed[h], h, 2)
    for h in range(2):
        steps[h, 1].wait_recv()
        acc[0, h] = acc[0, h] + near[h, 1]
    for h in range(2):
        steps[h, 2].wait_recv()
        sketch_ref[:, h * half : (h + 1) * half] = acc[0, h] + near[h, 2]

    quarter = half // 2

    def block(i, j0, j1):
        return lax.dot_general(
            sketch_ref[:, i * quarter : (i + 1) * quarter],
            sketch_ref[:, j0 * quarter : j1 * quarter],
            (((0,), (0,)), ((), ())),
            precision=lax.Precision.HIGHEST,
            preferred_element_type=F32,
        )

    value = block(0, 0, 4)
    gsum[0, 0:quarter, :] = value[:, :half]
    gsum[1, 0:quarter, :] = value[:, half:]
    value = block(1, 1, 4)
    gsum[0, quarter:half, quarter:half] = value[:, :quarter]
    gsum[1, quarter:half, :] = value[:, quarter:]
    gsum[0, quarter:half, 0:quarter] = block(3, 3, 4)
    value = block(2, 2, 4)
    gsum[0, half:, :] = value[: quarter // 2, :]
    gsum[1, half:, :] = value[quarter // 2 :, :]

    packed = gsum.shape[1]
    core_rows = packed // 2
    piece = packed // 8
    theirs = pl.ds(pl.multiple_of((1 - c) * core_rows, 8), core_rows)
    ours = pl.ds(pl.multiple_of(c * core_rows, 8), core_rows)
    got = [
        send(gsum.at[h, theirs], gcore.at[h], gcore_s.at[h], gcore_r.at[h], core_id)
        for h in range(2)
    ]

    def chip(dy, dx):
        cy = 1 - y if dy else y
        cx = 1 - x if dx else x
        return pl.multiple_of((cy * 2 + cx) * piece, 8)

    def rows_of(dy, dx):
        return pl.ds(chip(dy, dx), piece)

    def gnear_send(dy, dx, h, step):
        peer = second[h] if step == 2 else first[h]
        return send(
            gown.at[h, rows_of(dy, dx)], gnear.at[h, step], gnear_s.at[h, step], gnear_r.at[h, step], peer
        )

    passed_at = ((1, 0), (0, 1))
    direct_at = ((0, 1), (1, 0))
    for h in range(2):
        got[h].wait_recv()
        gown[h] = gsum[h, ours] + gcore[h]
        steps[h, 0] = gnear_send(1, 1, h, 0)
        steps[h, 1] = gnear_send(*direct_at[h], h, 1)
    for h in range(2):
        steps[h, 0].wait_recv()
        rows = rows_of(*passed_at[h])
        gown[h, rows] = gown[h, rows] + gnear[h, 0]
        steps[h, 2] = gnear_send(*passed_at[h], h, 2)
    mine = rows_of(0, 0)
    for h in range(2):
        steps[h, 1].wait_recv()
        steps[h, 2].wait_recv()
        gown[h, mine] = (gown[h, mine] + gnear[h, 1]) + gnear[h, 2]

    keep = lax.rem(z, 2)
    at = pl.ds(pl.multiple_of(c * core_rows + chip(0, 0), 8), piece)
    copy = send(gown.at[1 - keep, mine], gz.at[0], gz_s.at[0], gz_r.at[0], z_near_id)
    copy.wait_recv()
    gz[2] = gown[keep, mine] + gz[0]
    copy = send(gz.at[2], gz.at[1], gz_s.at[1], gz_r.at[1], z_far_id)
    copy.wait_recv()
    gall[keep, at] = gz[2] + gz[1]
    copy = send(gall.at[keep, at], gall.at[keep, at], gz_s.at[2], gz_r.at[2], z_near_id)
    pltpu.make_async_remote_copy(
        src_ref=gall.at[1 - keep, at], dst_ref=gall.at[1 - keep, at],
        send_sem=gz_s.at[2], recv_sem=gz_r.at[2], device_id=z_near_id, device_id_type=MESH,
    ).wait_recv()

    def place(dy, dx, core):
        return pl.ds(pl.multiple_of(core * core_rows + chip(dy, dx), 8), piece)

    def back(dy, dx, h, step, peer):
        ref = gall.at[h, place(dy, dx, c)]
        return send(ref, ref, gback_s.at[h, step], gback_r.at[h, step], peer)

    def pair(dy, dx, h, step):
        ref = gall.at[h, place(dy, dx, c)]
        return send(ref, ref, gpair_s.at[h, step], gpair_r.at[h, step], core_id)

    def landed(dy, dx, core, h, sems, step):
        ref = gall.at[h, place(dy, dx, core)]
        pltpu.make_async_remote_copy(
            src_ref=ref, dst_ref=ref, send_sem=gback_s.at[h, step], recv_sem=sems.at[h, step],
            device_id=core_id, device_id_type=MESH,
        ).wait_recv()

    along = ((1, 0), (0, 1))
    across = ((0, 1), (1, 0))
    for h in range(2):
        back(0, 0, h, 0, second[h])
        back(0, 0, h, 1, first[h])
    for h in range(2):
        pair(0, 0, h, 0)
    for h in range(2):
        landed(*along[h], c, h, gback_r, 0)
        back(*along[h], h, 2, first[h])
        pair(*along[h], h, 1)
    for h in range(2):
        landed(*across[h], c, h, gback_r, 1)
        pair(*across[h], h, 2)
    for h in range(2):
        landed(1, 1, c, h, gback_r, 2)
        pair(1, 1, h, 3)
    for h in range(2):
        landed(0, 0, 1 - c, h, gpair_r, 0)
        landed(*along[h], 1 - c, h, gpair_r, 1)
        landed(*across[h], 1 - c, h, gpair_r, 2)
        landed(1, 1, 1 - c, h, gpair_r, 3)
    gram_ref[...] = gall[...]
    for copy in pending:
        copy.wait_send()


def per_device_fast(design, scales, buckets):
    row_count, col_count = design.shape
    owned = row_count // lax.axis_size("row")
    half = col_count // 2
    packed = col_count // 4 * 5 // 2
    piece = packed // 8
    dma = pltpu.SemaphoreType.DMA
    vmem = pl.BlockSpec(memory_space=pltpu.VMEM)
    sketch, gram = pl.pallas_call(
        embed_kernel,
        out_shape=(
            jax.ShapeDtypeStruct((owned, col_count), F32),
            jax.ShapeDtypeStruct((2, packed, half), F32),
        ),
        in_specs=[vmem] * 3,
        out_specs=(vmem, vmem),
        scratch_shapes=[
            pltpu.VMEM((4, 2, owned, half), F32),
            pltpu.VMEM((4, 2, owned, half), F32),
            pltpu.VMEM((4, 2, owned, half), F32),
            pltpu.VMEM((2, 3, owned, half), F32),
            pltpu.VMEM((2, packed, half), F32),
            pltpu.VMEM((2, packed // 2, half), F32),
            pltpu.VMEM((2, packed // 2, half), F32),
            pltpu.VMEM((2, 3, piece, half), F32),
            pltpu.VMEM((3, piece, half), F32),
            pltpu.VMEM((2, packed, half), F32),
            dma((4,)), dma((4,)),
            dma((2, 3)), dma((2, 3)),
            dma((2,)), dma((2,)),
            dma((2, 3)), dma((2, 3)),
            dma((3,)), dma((3,)),
            dma((2, 3)), dma((2, 3)),
            dma((2, 4)), dma((2, 4)),
        ],
        compiler_params=pltpu.CompilerParams(
            collective_id=0, has_side_effects=True, vmem_limit_bytes=40 * 1024 * 1024
        ),
        name="embed",
    )(design, scales.astype(F32).reshape(1, row_count), buckets.reshape(1, row_count))
    grp_count = lax.axis_size("grp")
    scale = 1.0 / math.sqrt(row_count * grp_count)
    slab = factor_call(factor_kernel, gram, col_count, col_count // grp_count, scale)
    return (sketch, slab)


def solution(mesh):
    in_specs = (P(("grp", "row"), None), P(("grp", "row")), P(("grp", "row")))
    out_specs = (P(("grp", "row"), None), P("grp", None))
    fast = mesh.shape["grp"] == 4 and mesh.shape["row"] == 8
    return jax.shard_map(
        per_device_fast if fast else per_device_general,
        mesh=mesh, in_specs=in_specs, out_specs=out_specs, check_vma=False,
    )
```

time: 289 us -> 66.3 us (0.23)
  waiting for transfers between devices: 129 us -> 0 us
  other arithmetic: 83.4 us -> 0 us
  Pallas kernels: 0 us -> 61.9 us
  blocking collectives: 42.9 us -> 0 us
  between operations: 16.7 us -> 0.64 us
  matrix products: 10.9 us -> 0 us
    psum x1 -> x0, waiting for transfers between devices: 129 us -> none  [per_device(): whole_gram = lax.psum(local_gram, ('grp', 'row'))]
    another operation x14 -> x0, other arithmetic: 78.6 us -> none  [chol_upper(): return jnp.linalg.cholesky(gram_matrix).T]
    pallas_call x0 -> x2, Pallas kernels: none -> 61.9 us  [the longest x1 47.1 us: per_device_fast(): pl.pallas_call(embed_kernel, out_shape=(jax.ShapeDtypeStruct((owned, col_...]
    all_to_all x1 -> x0, blocking collectives: 42.9 us -> none  [per_device(): lax.all_to_all(partial_value, 'row', split_axis=0, concat_axis=0, tiled=T...]
    another operation x6 -> x0, matrix products: 5.46 us -> none  [chol_upper(): return jnp.linalg.cholesky(gram_matrix).T]
    dot_general x2 -> x0, matrix products: 5.45 us -> none  [the longest x1 3.31 us: per_device(): jnp.dot(onehot_table, design, preferred_element_type=jnp.float32)]
  transfers between devices with their start and end apart: 1 -> 0, of which waited for: 1 -> 0; matrix products, arithmetic and copies ran while one was open for 0% -> 0% of each run, Pallas kernels for 0% -> 0%
where the time goes in v1:
time: 66.3 us; the launch traced here: 66.1 us
  Pallas kernels  61.9 us (93%)
  local copies, waits for them, and re-layouts  3.55 us (5%)
    pallas_call x1, Pallas kernels, per_device_fast(): pl.pallas_call(embed_kernel, out_shape=(jax.ShapeDtypeStruct((owned, col_...  47.1 us
    pallas_call x1, Pallas kernels, factor_call(): pl.pallas_call(functools.partial(kernel, scale), out_shape=jax.ShapeDtype...  14.8 us
    unnamed x3, local copies, waits for them, and re-layouts  2.15 us

profile of v1, /device:TPU:0, one launch (start us, length us, event | category | flops | bytes accessed | tf_op | source)
XLA Modules:
  0.0 66.1 jit_solution(12489070792710678643)
XLA Ops:
  0.6 0.7 %reshape.17.buckets_ref = s32[1,1536]{1,0:T(1,128)S(1)} reshape(s32[1536]{0:T(1024)} %param.5) | data formatting | bytes 12288 | tf_op jit(solution)/shard_map/reshape | solution.py:410
  1.3 0.7 %reshape.20.scales_ref = f32[1,1536]{1,0:T(1,128)S(1)} reshape(bf16[1536]{0:T(1024)(128)(2,1)} %param.4) | data formatting | bytes 9216 | tf_op jit(solution)/shard_map/reshape | solution.py:410
  2.0 0.0 copy-start
  2.0 1.4 %copy-done = bf16[1536,512]{1,0:T(8,128)(2,1)S(1)} copy-done((bf16[1536,512]{1,0:T(8,128)(2,1)S(1)}, bf16[1536,512]{1,0:T(8,128)(2,1)}, u32[]{:S(2)}) %copy-start) | copy-done | bytes 1572888
  3.4 47.1 %embed.1 = (f32[192,512]{1,0:T(8,128)S(1)}, f32[2,320,256]{2,1,0:T(8,128)S(1)}) custom-call(bf16[1536,512]{1,0:T(8,128)(2,1)S(1)} %copy-done, f32[1,1536]{1,0:T(1,128)S(1)} %reshape.20.scales_ref, s32[1,1536]{1,0:T(1,128)S(1)} %reshape.17.buckets_ref), custom_call_target="tpu_custom_call" | custom-call | tf_op jit(solution)/shard_map/embed/pallas_call | solution.py:379
  50.5 14.8 %factor.1 = f32[128,512]{1,0:T(8,128)} custom-call(s32[1]{0:T(128)} %bitcast.grp_ref, f32[2,320,256]{2,1,0:T(8,128)S(1)} %get-tuple-element.5.gram_ref), custom_call_target="tpu_custom_call" | custom-call | tf_op jit(solution)/shard_map/factor/pallas_call | solution.py:116
  65.3 0.7 %copy.6 = f32[192,512]{1,0:T(8,128)} copy(f32[192,512]{1,0:T(8,128)S(1)} %get-tuple-element.8) | data formatting | bytes 786432
Async XLA Ops:
  2.0 1.4 %copy-start = (bf16[1536,512]{1,0:T(8,128)(2,1)S(1)}, bf16[1536,512]{1,0:T(8,128)(2,1)}, u32[]{:S(2)}) copy-start(bf16[1536,512]{1,0:T(8,128)(2,1)} %design_ref.1) | copy-start | bytes 4718596

commit v2 on v1

--- a/solution.py
+++ b/solution.py
@@ -44,8 +44,10 @@
     return [part * scale for part in parts]
 
 
-def factor_kernel(scale, grp_ref, gram_ref, out_ref, work):
+def factor_kernel(scale, grp_ref, gram_ref, sketch_ref, out_ref, sketch_out, work, copy_sem):
     size = work.shape[0]
+    copy = pltpu.make_async_copy(sketch_ref, sketch_out, copy_sem)
+    copy.start()
     half = size // 2
     quarter = size // 4
     for h in range(2):
@@ -58,6 +60,7 @@
     work[half + quarter // 2 : 3 * quarter, half:size] = gram_ref[1, half : half + quarter // 2, :]
     factor_in_place(work)
     write_rows(scale, grp_ref, out_ref, work)
+    copy.wait()
 
 
 def factor_whole_kernel(scale, grp_ref, gram_ref, out_ref, work):
@@ -110,21 +113,23 @@
     out_ref[...] = jnp.where(cols >= rows, value, 0.0)
 
 
-def factor_call(kernel, gram, size, slab_rows, scale):
+def factor_call(kernel, gram, size, slab_rows, scale, sketch=None):
+    anywhere = pl.BlockSpec(memory_space=pl.ANY)
+    vmem = pl.BlockSpec(memory_space=pltpu.VMEM)
+    smem = pl.BlockSpec(memory_space=pltpu.SMEM)
+    slab_shape = jax.ShapeDtypeStruct((slab_rows, size), F32)
+    carried = sketch is not None
     grp = lax.axis_index("grp").astype(jnp.int32).reshape((1,))
 
     return pl.pallas_call(
         functools.partial(kernel, scale),
-        out_shape=jax.ShapeDtypeStruct((slab_rows, size), F32),
-        in_specs=[
-            pl.BlockSpec(memory_space=pltpu.SMEM),
-            pl.BlockSpec(memory_space=pltpu.VMEM),
-        ],
-        out_specs=pl.BlockSpec(memory_space=pltpu.VMEM),
-        scratch_shapes=[pltpu.VMEM((size, size), F32)],
+        out_shape=(slab_shape, jax.ShapeDtypeStruct(sketch.shape, F32)) if carried else slab_shape,
+        in_specs=[smem, vmem, anywhere] if carried else [smem, vmem],
+        out_specs=(vmem, anywhere) if carried else vmem,
+        scratch_shapes=[pltpu.VMEM((size, size), F32)] + [pltpu.SemaphoreType.DMA] * carried,
         compiler_params=pltpu.CompilerParams(vmem_limit_bytes=32 * 1024 * 1024),
         name="factor",
-    )(grp, gram)
+    )(grp, gram, *([sketch] if carried else []))
 
 
 def self_gram(matrix):
@@ -159,8 +164,8 @@
 
 
 def embed_kernel(
-    design_ref, scales_ref, buckets_ref, sketch_ref, gram_ref,
-    give, took, acc, near, gsum, gcore, gown, gnear, gz, gall,
+    design_hbm, scales_ref, buckets_ref, sketch_ref, gram_ref,
+    design_ref, load_s, give, took, acc, near, gsum, gcore, gown, gnear, gz, gall,
     give_s, give_r, near_s, near_r, gcore_s, gcore_r, gnear_s, gnear_r, gz_s, gz_r,
     gback_s, gback_r, gpair_s, gpair_r,
 ):
@@ -179,7 +184,8 @@
     barrier = pltpu.get_barrier_semaphore()
     for peer in peers:
         pl.semaphore_signal(barrier, inc=1, device_id=peer, device_id_type=MESH)
-    pl.semaphore_wait(barrier, len(peers))
+    load = pltpu.make_async_copy(design_hbm, design_ref, load_s)
+    load.start()
 
     pending = []
 
@@ -196,25 +202,23 @@
     owned = sketch_ref.shape[0]
     half = design_ref.shape[1] // 2
 
-    def part(slot, core):
+    def part(slot):
         ty = y if slot < 2 else 1 - y
         tx = x if slot % 2 == 0 else 1 - x
-        base = (ty * 4 + tx * 2 + core) * owned
-        labels = base + lax.broadcasted_iota(jnp.int32, (owned, rows_all), 0)
-        table = jnp.where(labels == buckets_ref[...], scales_ref[...], 0.0).astype(BF16)
-        return jnp.dot(table, design_ref[...], preferred_element_type=F32)
-
-    order = (3, 2, 1, 0)
-    from_core = {}
-    for s in order:
-        value = part(s, 1 - c)
-        give[s, 0] = value[:, :half]
-        give[s, 1] = value[:, half:]
-        from_core[s] = send(give.at[s], took.at[s], give_s.at[s], give_r.at[s], core_id)
-    for s in order:
-        value = part(s, c)
-        acc[s, 0] = value[:, :half]
-        acc[s, 1] = value[:, half:]
+        base = (ty * 4 + tx * 2) * owned
+        ids = lax.broadcasted_iota(jnp.int32, (owned, LANES), 0) + base
+        labels = jnp.concatenate([ids + (1 - c) * owned, ids + c * owned], axis=0)
+        table = jnp.concatenate(
+            [
+                jnp.where(labels == buckets_ref[k : k + 1, :], scales_ref[k : k + 1, :], 0.0).astype(BF16)
+                for k in range(rows_all // LANES)
+            ],
+            axis=1,
+        )
+        value = jnp.dot(table, design_ref[...], preferred_element_type=F32)
+        for h in range(2):
+            give[slot, h] = value[:owned, h * half : (h + 1) * half]
+            acc[slot, h] = value[owned:, h * half : (h + 1) * half]
 
     first = (x_id, y_id)
     second = (y_id, x_id)
@@ -226,14 +230,35 @@
         return send(acc.at[slot, h], near.at[h, step], near_s.at[h, step], near_r.at[h, step], peer)
 
     steps = {}
-    for s in order:
-        from_core[s].wait_recv()
+    from_core = {}
+    order = (3, 2, 1, 0)
+
+    def give_core(slot):
+        from_core[slot] = send(give.at[slot], took.at[slot], give_s.at[slot], give_r.at[slot], core_id)
+
+    def take_core(slot):
+        from_core[slot].wait_recv()
         for h in range(2):
-            acc[s, h] = acc[s, h] + took[s, h]
-            if s == 3:
-                steps[h, 0] = near_send(3, h, 0)
-            elif s == direct[h]:
-                steps[h, 1] = near_send(s, h, 1)
+            acc[slot, h] = acc[slot, h] + took[slot, h]
+            if slot == 3:
+                steps[h, 0] = near_send(slot, h, 0)
+            elif slot == direct[h]:
+                steps[h, 1] = near_send(slot, h, 1)
+
+    load.wait()
+    part(3)
+    pl.semaphore_wait(barrier, len(peers))
+    give_core(3)
+    part(2)
+    give_core(2)
+    take_core(3)
+    part(1)
+    give_core(1)
+    take_core(2)
+    part(0)
+    give_core(0)
+    take_core(1)
+    take_core(0)
     for h in range(2):
         steps[h, 0].wait_recv()
         acc[passed[h], h] = acc[passed[h], h] + near[h, 0]
@@ -382,9 +407,11 @@
             jax.ShapeDtypeStruct((owned, col_count), F32),
             jax.ShapeDtypeStruct((2, packed, half), F32),
         ),
-        in_specs=[vmem] * 3,
+        in_specs=[pl.BlockSpec(memory_space=pl.ANY), vmem, vmem],
         out_specs=(vmem, vmem),
         scratch_shapes=[
+            pltpu.VMEM((row_count, col_count), BF16),
+            pltpu.SemaphoreType.DMA,
             pltpu.VMEM((4, 2, owned, half), F32),
             pltpu.VMEM((4, 2, owned, half), F32),
             pltpu.VMEM((4, 2, owned, half), F32),
@@ -404,13 +431,13 @@
             dma((2, 4)), dma((2, 4)),
         ],
         compiler_params=pltpu.CompilerParams(
-            collective_id=0, has_side_effects=True, vmem_limit_bytes=40 * 1024 * 1024
+            collective_id=0, has_side_effects=True, vmem_limit_bytes=60 * 1024 * 1024
         ),
         name="embed",
-    )(design, scales.astype(F32).reshape(1, row_count), buckets.reshape(1, row_count))
+    )(design, scales.astype(F32).reshape(-1, LANES), buckets.reshape(-1, LANES))
     grp_count = lax.axis_size("grp")
     scale = 1.0 / math.sqrt(row_count * grp_count)
-    slab = factor_call(factor_kernel, gram, col_count, col_count // grp_count, scale)
+    slab, sketch = factor_call(factor_kernel, gram, col_count, col_count // grp_count, scale, sketch)
     return (sketch, slab)
 
 

time: 66.3 us -> 68.3 us (1.030)
  Pallas kernels: 61.9 us -> 64 us
  local copies, waits for them, and re-layouts: 3.55 us -> 2.08 us
  other arithmetic: 0 us -> 1.29 us
    pallas_call x1, Pallas kernels: 47.1 us -> 49.1 us  [per_device_fast(): pl.pallas_call(embed_kernel, out_shape=(jax.ShapeDtypeStruct((owned, col_...]
    reshape x2 -> x0, local copies, waits for them, and re-layouts: 1.39 us -> none  [the longest x1 0.7 us: per_device_fast(): buckets.reshape(1, row_count)]
    reshape x0 -> x1, other arithmetic: none -> 1.29 us  [per_device_fast(): scales.astype(F32).reshape(-1, LANES)]
    unnamed x3 -> x4, local copies, waits for them, and re-layouts: 2.15 us -> 2.08 us
where the time goes in v2:
time: 68.3 us; the launch traced here: 68 us
  Pallas kernels  64 us (94%)
  local copies, waits for them, and re-layouts  2.08 us (3%)
  other arithmetic  1.29 us (2%)
    pallas_call x1, Pallas kernels, per_device_fast(): pl.pallas_call(embed_kernel, out_shape=(jax.ShapeDtypeStruct((owned, col_...  49.1 us
    pallas_call x1, Pallas kernels, factor_call(): pl.pallas_call(functools.partial(kernel, scale), out_shape=(slab_shape, j...  14.8 us
    unnamed x4, local copies, waits for them, and re-layouts  2.08 us

profile of v2, /device:TPU:0, one launch (start us, length us, event | category | flops | bytes accessed | tf_op | source)
XLA Modules:
  0.0 68.0 jit_solution(17738630153611318942)
XLA Ops:
  0.6 1.3 %bitcast_convert_fusion.scales_ref = f32[12,128]{1,0:T(8,128)} fusion(bf16[1536]{0:T(1024)(128)(2,1)} %param.4), kind=kLoop, calls=%fused_computation | loop fusion | flops 1536 | bytes 9216 | tf_op jit(solution)/shard_map/reshape | solution.py:437
  1.9 49.1 %embed.1 = (f32[192,512]{1,0:T(8,128)}, f32[2,320,256]{2,1,0:T(8,128)}) custom-call(bf16[1536,512]{1,0:T(8,128)(2,1)} %design_hbm.1, f32[12,128]{1,0:T(8,128)} %bitcast_convert_fusion.scales_ref, s32[12,128]{1,0:T(8,128)} %bitcast.5), custom_call_target="tpu_custom_call" | custom-call | tf_op jit(solution)/shard_map/embed/pallas_call | solution.py:404
  51.1 0.0 copy-start
  51.1 1.1 %copy-done = f32[2,320,256]{2,1,0:T(8,128)S(1)} copy-done((f32[2,320,256]{2,1,0:T(8,128)S(1)}, f32[2,320,256]{2,1,0:T(8,128)}, u32[]{:S(2)}) %copy-start) | copy-done | bytes 655384
  52.2 0.0 copy-start.1
  52.2 1.0 %copy-done.1 = f32[192,512]{1,0:T(8,128)S(1)} copy-done((f32[192,512]{1,0:T(8,128)S(1)}, f32[192,512]{1,0:T(8,128)}, u32[]{:S(2)}) %copy-start.1) | copy-done | bytes 393240
  53.2 14.8 %factor.1 = (f32[128,512]{1,0:T(8,128)}, f32[192,512]{1,0:T(8,128)}) custom-call(s32[1]{0:T(128)} %bitcast.grp_ref, f32[2,320,256]{2,1,0:T(8,128)S(1)} %copy-done, f32[192,512]{1,0:T(8,128)S(1)} %copy-done.1), custom_call_target="tpu_custom_call" | custom-call | tf_op jit(solution)/shard_map/factor/pallas_call | solution.py:124
Async XLA Ops:
  51.1 1.1 %copy-start = (f32[2,320,256]{2,1,0:T(8,128)S(1)}, f32[2,320,256]{2,1,0:T(8,128)}, u32[]{:S(2)}) copy-start(f32[2,320,256]{2,1,0:T(8,128)} %get-tuple-element.6.gram_ref) | copy-start | bytes 1966084
  52.2 1.0 %copy-start.1 = (f32[192,512]{1,0:T(8,128)S(1)}, f32[192,512]{1,0:T(8,128)}, u32[]{:S(2)}) copy-start(f32[192,512]{1,0:T(8,128)} %get-tuple-element.7.sketch_ref) | copy-start | bytes 1179652

commit v3 on v0

v3 whole, which is shorter than its diff:
```python
import functools
import math

import jax
import jax.numpy as jnp
from jax import lax
from jax.experimental import pallas as pl
from jax.experimental.pallas import tpu as pltpu
from jax.sharding import PartitionSpec as P

MESH = pl.DeviceIdType.MESH
F32 = jnp.float32
BF16 = jnp.bfloat16
LANES = 128
PANEL = 16


def split3(value):
    high = value.astype(BF16)
    rest = value - high.astype(F32)
    mid = rest.astype(BF16)
    low = (rest - mid.astype(F32)).astype(BF16)
    return high, mid, low


def panel_factor(panel, offset):
    size, width = panel.shape
    tiles = width // LANES
    sub = lax.broadcasted_iota(jnp.int32, (size, LANES), 0)
    cols = [
        jnp.broadcast_to(panel[:, offset + k : offset + k + 1], (size, LANES))
        for k in range(size)
    ]
    parts = [panel[:, t * LANES : (t + 1) * LANES] for t in range(tiles)]
    scale = jnp.zeros((size, LANES), F32)
    for j in range(size):
        inv = lax.rsqrt(cols[j][j : j + 1, :])
        mult = cols[j] * inv
        scale = jnp.where(sub == j, inv, scale)
        for k in range(j + 1, size):
            cols[k] = cols[k] - mult * (cols[k][j : j + 1, :] * inv)
        below = jnp.where(sub > j, mult, 0.0)
        parts = [part - below * (part[j : j + 1, :] * inv) for part in parts]
    return [part * scale for part in parts]


def factor_block(work, base, stop, hook=None):
    for start in range(0, LANES, PANEL):
        row = base + start
        rows = panel_factor(work[row : row + PANEL, base:stop], start)
        for t, part in enumerate(rows):
            work[row : row + PANEL, base + t * LANES : base + (t + 1) * LANES] = part
        if hook is not None:
            hook()
        if start + PANEL == LANES:
            break
        splits = [split3(part) for part in rows]
        h, m, l = splits[0]
        lhs = jnp.concatenate([h, h, m, h, l, m], axis=0)
        for t, (h, m, l) in enumerate(splits):
            rhs = jnp.concatenate([h, m, h, l, h, m], axis=0)
            prod = lax.dot_general(lhs, rhs, (((0,), (0,)), ((), ())), preferred_element_type=F32)
            cs = slice(base + t * LANES, base + (t + 1) * LANES)
            work[row + PANEL : base + LANES, cs] = (
                work[row + PANEL : base + LANES, cs] - prod[start + PANEL :, :]
            )


def tdot(left, right):
    return lax.dot_general(
        left, right, (((0,), (0,)), ((), ())),
        precision=lax.Precision.HIGHEST, preferred_element_type=F32,
    )


def trail(work, base, last, stop):
    for left in range(base + LANES, last, LANES):
        work[left : left + LANES, left:stop] = work[left : left + LANES, left:stop] - tdot(
            work[base : base + LANES, left : left + LANES], work[base : base + LANES, left:stop]
        )


def write_rows(grp, scale, out_ref, work):
    size = work.shape[0]
    count = out_ref.shape[0]
    first = pl.multiple_of(grp * count, count)
    rows = first + lax.broadcasted_iota(jnp.int32, (count, size), 0)
    cols = lax.broadcasted_iota(jnp.int32, (count, size), 1)
    value = work[pl.ds(first, count), :] * scale
    out_ref[...] = jnp.where(cols >= rows, value, 0.0)


def factor_kernel(scale, gram_ref, out_ref, work):
    size = work.shape[0]
    work[...] = gram_ref[...]
    for base in range(0, size, LANES):
        factor_block(work, base, size)
        trail(work, base, size, size)
    write_rows(lax.axis_index("grp"), scale, out_ref, work)


def factor_call(gram, slab_rows, scale):
    size = gram.shape[0]
    vmem = pl.BlockSpec(memory_space=pltpu.VMEM)
    return pl.pallas_call(
        functools.partial(factor_kernel, scale),
        out_shape=jax.ShapeDtypeStruct((slab_rows, size), F32),
        in_specs=[vmem],
        out_specs=vmem,
        scratch_shapes=[pltpu.VMEM((size, size), F32)],
        compiler_params=pltpu.CompilerParams(vmem_limit_bytes=32 * 1024 * 1024),
        name="factor",
    )(gram)


def self_gram(matrix):
    return lax.dot_general(
        matrix,
        matrix,
        (((0,), (0,)), ((), ())),
        precision=lax.Precision.HIGHEST,
        preferred_element_type=F32,
    )


def per_device_general(design, scales, buckets):
    row_count = design.shape[0]
    col_count = design.shape[1]
    row_parts = lax.axis_size("row")
    owned_rows = row_count // row_parts
    label_ids = lax.iota(jnp.int32, row_count)
    onehot_table = jnp.where(
        label_ids[:, None] == buckets[None, :], scales[None, :], jnp.zeros((), BF16)
    )
    partial_value = jnp.dot(onehot_table, design, preferred_element_type=F32).reshape(
        row_parts, owned_rows, col_count
    )
    arrived = lax.all_to_all(partial_value, "row", split_axis=0, concat_axis=0, tiled=True)
    sketch = jnp.sum(arrived, axis=0)
    whole_gram = lax.psum(self_gram(sketch), ("grp", "row"))
    grp_count = lax.axis_size("grp")
    scale = 1.0 / math.sqrt(row_count * grp_count)
    slab = factor_call(whole_gram, col_count // grp_count, scale)
    return (sketch, slab)


def embed_kernel(
    scale, design_hbm, scales_in, buckets_ref, sketch_out, out_ref,
    design_ref, load_s, sketch_ref, store_s, scales_ref, work,
    give, took, acc, near, give_s, give_r, near_s, near_r, *chunk_refs,
):
    z = lax.axis_index("grp")
    row = lax.axis_index("row")
    c = lax.rem(row, 2)
    x = lax.rem(row // 2, 2)
    y = row // 4
    core_id = (z, row + 1 - 2 * c)
    x_id = (z, row + 2 - 4 * x)
    y_id = (z, row + 4 - 8 * y)
    z_near_id = (z + 1 - 2 * lax.rem(z, 2), row)
    z_far_id = (z + 2 - 4 * (z // 2), row)
    peers = (core_id, x_id, y_id, z_near_id, z_far_id)

    barrier = pltpu.get_barrier_semaphore()
    for peer in peers:
        pl.semaphore_signal(barrier, inc=1, device_id=peer, device_id_type=MESH)
    load = pltpu.make_async_copy(design_hbm, design_ref, load_s)
    load.start()

    pending = []

    def send(src, dst, send_sem, recv_sem, peer):
        copy = pltpu.make_async_remote_copy(
            src_ref=src, dst_ref=dst, send_sem=send_sem, recv_sem=recv_sem,
            device_id=peer, device_id_type=MESH,
        )
        copy.start()
        pending.append(copy)
        return copy

    scales_ref[...] = scales_in[...].astype(F32)
    work[...] = jnp.zeros_like(work)
    rows_all = design_ref.shape[0]
    owned = sketch_ref.shape[0]
    half = design_ref.shape[1] // 2

    def part(slot):
        ty = y if slot < 2 else 1 - y
        tx = x if slot % 2 == 0 else 1 - x
        base = (ty * 4 + tx * 2) * owned
        ids = lax.broadcasted_iota(jnp.int32, (owned, LANES), 0) + base
        labels = jnp.concatenate([ids + (1 - c) * owned, ids + c * owned], axis=0)
        table = jnp.concatenate(
            [
                jnp.where(labels == buckets_ref[k : k + 1, :], scales_ref[k : k + 1, :], 0.0).astype(BF16)
                for k in range(rows_all // LANES)
            ],
            axis=1,
        )
        value = jnp.dot(table, design_ref[...], preferred_element_type=F32)
        for h in range(2):
            give[slot, h] = value[:owned, h * half : (h + 1) * half]
            acc[slot, h] = value[owned:, h * half : (h + 1) * half]

    first = (x_id, y_id)
    second = (y_id, x_id)
    passed = (2, 1)
    direct = (1, 2)

    def near_send(slot, h, step):
        peer = second[h] if step == 2 else first[h]
        return send(acc.at[slot, h], near.at[h, step], near_s.at[h, step], near_r.at[h, step], peer)

    steps = {}
    from_core = {}
    order = (3, 2, 1, 0)

    def give_core(slot):
        from_core[slot] = send(give.at[slot], took.at[slot], give_s.at[slot], give_r.at[slot], core_id)

    def take_core(slot):
        from_core[slot].wait_recv()
        for h in range(2):
            acc[slot, h] = acc[slot, h] + took[slot, h]
            if slot == 3:
                steps[h, 0] = near_send(slot, h, 0)
            elif slot == direct[h]:
                steps[h, 1] = near_send(slot, h, 1)

    load.wait()
    part(3)
    pl.semaphore_wait(barrier, len(peers))
    give_core(3)
    part(2)
    give_core(2)
    take_core(3)
    part(1)
    give_core(1)
    take_core(2)
    part(0)
    give_core(0)
    take_core(1)
    take_core(0)
    for h in range(2):
        steps[h, 0].wait_recv()
        acc[passed[h], h] = acc[passed[h], h] + near[h, 0]
        steps[h, 2] = near_send(passed[h], h, 2)
    for h in range(2):
        steps[h, 1].wait_recv()
        acc[0, h] = acc[0, h] + near[h, 1]
    for h in range(2):
        steps[h, 2].wait_recv()
        sketch_ref[:, h * half : (h + 1) * half] = acc[0, h] + near[h, 2]

    store = pltpu.make_async_copy(sketch_ref, sketch_out, store_s)
    store.start()

    def chip(dy, dx, piece):
        cy = 1 - y if dy else y
        cx = 1 - x if dx else x
        return pl.multiple_of((cy * 2 + cx) * piece, 8)

    passed_at = ((1, 0), (0, 1))
    direct_at = ((0, 1), (1, 0))

    def all_reduce(refs):
        (gsum, gcore, gown, gnear, gz, gall, gcore_s, gcore_r, gnear_s, gnear_r,
         gz_s, gz_r, gback_s, gback_r, gpair_s, gpair_r) = refs
        packed = gsum.shape[1]
        core_rows = packed // 2
        piece = packed // 8
        theirs = pl.ds(pl.multiple_of((1 - c) * core_rows, 8), core_rows)
        ours = pl.ds(pl.multiple_of(c * core_rows, 8), core_rows)
        got = [
            send(gsum.at[h, theirs], gcore.at[h], gcore_s.at[h], gcore_r.at[h], core_id)
            for h in range(2)
        ]
        yield

        def rows_of(dy, dx):
            return pl.ds(chip(dy, dx, piece), piece)

        def gnear_send(dy, dx, h, step):
            peer = second[h] if step == 2 else first[h]
            return send(
                gown.at[h, rows_of(dy, dx)], gnear.at[h, step],
                gnear_s.at[h, step], gnear_r.at[h, step], peer,
            )

        hops = {}
        for h in range(2):
            got[h].wait_recv()
            gown[h] = gsum[h, ours] + gcore[h]
            hops[h, 0] = gnear_send(1, 1, h, 0)
            hops[h, 1] = gnear_send(*direct_at[h], h, 1)
        yield
        for h in range(2):
            hops[h, 0].wait_recv()
            rows = rows_of(*passed_at[h])
            gown[h, rows] = gown[h, rows] + gnear[h, 0]
            hops[h, 2] = gnear_send(*passed_at[h], h, 2)
        yield
        mine = rows_of(0, 0)
        for h in range(2):
            hops[h, 1].wait_recv()
            hops[h, 2].wait_recv()
            gown[h, mine] = (gown[h, mine] + gnear[h, 1]) + gnear[h, 2]

        keep = lax.rem(z, 2)
        at = pl.ds(pl.multiple_of(c * core_rows + chip(0, 0, piece), 8), piece)
        copy = send(gown.at[1 - keep, mine], gz.at[0], gz_s.at[0], gz_r.at[0], z_near_id)
        yield
        copy.wait_recv()
        gz[2] = gown[keep, mine] + gz[0]
        copy = send(gz.at[2], gz.at[1], gz_s.at[1], gz_r.at[1], z_far_id)
        yield
        copy.wait_recv()
        gall[keep, at] = gz[2] + gz[1]
        send(gall.at[keep, at], gall.at[keep, at], gz_s.at[2], gz_r.at[2], z_near_id)
        yield
        pltpu.make_async_remote_copy(
            src_ref=gall.at[1 - keep, at], dst_ref=gall.at[1 - keep, at],
            send_sem=gz_s.at[2], recv_sem=gz_r.at[2], device_id=z_near_id, device_id_type=MESH,
        ).wait_recv()

        def place(dy, dx, core):
            return pl.ds(pl.multiple_of(core * core_rows + chip(dy, dx, piece), 8), piece)

        def back(dy, dx, h, step, peer):
            ref = gall.at[h, place(dy, dx, c)]
            return send(ref, ref, gback_s.at[h, step], gback_r.at[h, step], peer)

        def pair(dy, dx, h, step):
            ref = gall.at[h, place(dy, dx, c)]
            return send(ref, ref, gpair_s.at[h, step], gpair_r.at[h, step], core_id)

        def landed(dy, dx, core, h, sems, step):
            ref = gall.at[h, place(dy, dx, core)]
            pltpu.make_async_remote_copy(
                src_ref=ref, dst_ref=ref, send_sem=gback_s.at[h, 0], recv_sem=sems.at[h, step],
                device_id=core_id, device_id_type=MESH,
            ).wait_recv()

        for h in range(2):
            back(0, 0, h, 0, second[h])
            back(0, 0, h, 1, first[h])
        for h in range(2):
            pair(0, 0, h, 0)
        yield
        for h in range(2):
            landed(*passed_at[h], c, h, gback_r, 0)
            back(*passed_at[h], h, 2, first[h])
            pair(*passed_at[h], h, 1)
        yield
        for h in range(2):
            landed(*direct_at[h], c, h, gback_r, 1)
            pair(*direct_at[h], h, 2)
        for h in range(2):
            landed(1, 1, c, h, gback_r, 2)
            pair(1, 1, h, 3)
        yield
        for h in range(2):
            landed(0, 0, 1 - c, h, gpair_r, 0)
            landed(*passed_at[h], 1 - c, h, gpair_r, 1)
            landed(*direct_at[h], 1 - c, h, gpair_r, 2)
            landed(1, 1, 1 - c, h, gpair_r, 3)

    q = half // 2
    chunk_a, chunk_b = chunk_refs[:16], chunk_refs[16:]

    def cut(i, j=None):
        return sketch_ref[:, i * q : (i + 1 if j is None else j) * q]

    gsum = chunk_a[0]
    value = tdot(cut(0), cut(0, 2))
    gsum[0, 0:q] = value[:, :q]
    gsum[1, 0:q] = value[:, q:]
    value = tdot(cut(1), cut(1))
    gsum[0, q:] = value[: q // 2]
    gsum[1, q:] = value[q // 2 :]
    steps_a = all_reduce(chunk_a)
    next(steps_a)
    gsum = chunk_b[0]
    for i in range(3):
        value = tdot(cut(i), cut(2, 4))
        gsum[0, i * q : (i + 1) * q] = value[:, :q]
        gsum[1, i * q : (i + 1) * q] = value[:, q:]
    value = tdot(cut(3), cut(3))
    gsum[0, 3 * q :] = value[: q // 2]
    gsum[1, 3 * q :] = value[q // 2 :]
    steps_b = all_reduce(chunk_b)

    def run(steps, count=1):
        for _ in range(count):
            next(steps, None)

    run(steps_b)
    for _ in range(4):
        run(steps_a, 2)
        run(steps_b)
    run(steps_a, 2)

    gall = chunk_a[5]
    work[0:q, 0:q] = gall[0, 0:q]
    work[0:q, q:half] = gall[1, 0:q]
    work[q : q + q // 2, q:half] = gall[0, q:]
    work[q + q // 2 : half, q:half] = gall[1, q:]
    eye = (
        lax.broadcasted_iota(jnp.int32, (q, q), 0) == lax.broadcasted_iota(jnp.int32, (q, q), 1)
    ).astype(F32)
    work[0:q, half : half + q] = eye
    work[q:half, half + q :] = eye
    calls = []

    def hook():
        calls.append(0)
        if len(calls) % 2 == 0:
            run(steps_b)

    factor_block(work, 0, half + q, hook)
    trail(work, 0, half, half + q)
    factor_block(work, q, 2 * half, hook)
    for _ in steps_b:
        pass

    gall = chunk_b[5]
    right = jnp.concatenate([gall[0, :half], gall[1, :half]], axis=1)
    solved = lax.dot_general(
        work[0:half, half:], right, (((1,), (0,)), ((), ())),
        precision=lax.Precision.HIGHEST, preferred_element_type=F32,
    )
    work[0:half, half:] = solved
    prod = tdot(solved, solved)
    work[half : half + q, half : half + q] = gall[0, half : half + q] - prod[:q, :q]
    work[half : half + q, half + q :] = gall[1, half : half + q] - prod[:q, q:]
    work[half + q : half + q + q // 2, half + q :] = gall[0, 3 * q :] - prod[q : q + q // 2, q:]
    work[half + q + q // 2 :, half + q :] = gall[1, 3 * q :] - prod[q + q // 2 :, q:]
    factor_block(work, half, 2 * half)
    trail(work, half, 2 * half, 2 * half)
    factor_block(work, half + q, 2 * half)
    write_rows(z, scale, out_ref, work)
    store.wait()
    for copy in pending:
        copy.wait_send()


def chunk_scratch(packed, lanes):
    piece = packed // 8
    dma = pltpu.SemaphoreType.DMA
    return [
        pltpu.VMEM((2, packed, lanes), F32),
        pltpu.VMEM((2, packed // 2, lanes), F32),
        pltpu.VMEM((2, packed // 2, lanes), F32),
        pltpu.VMEM((2, 3, piece, lanes), F32),
        pltpu.VMEM((3, piece, lanes), F32),
        pltpu.VMEM((2, packed, lanes), F32),
        dma((2,)), dma((2,)),
        dma((2, 3)), dma((2, 3)),
        dma((3,)), dma((3,)),
        dma((2, 3)), dma((2, 3)),
        dma((2, 4)), dma((2, 4)),
    ]


def per_device_fast(design, scales, buckets):
    row_count, col_count = design.shape
    owned = row_count // lax.axis_size("row")
    half = col_count // 2
    quarter = half // 2
    grp_count = lax.axis_size("grp")
    dma = pltpu.SemaphoreType.DMA
    vmem = pl.BlockSpec(memory_space=pltpu.VMEM)
    return pl.pallas_call(
        functools.partial(embed_kernel, 1.0 / math.sqrt(row_count * grp_count)),
        out_shape=(
            jax.ShapeDtypeStruct((owned, col_count), F32),
            jax.ShapeDtypeStruct((col_count // grp_count, col_count), F32),
        ),
        in_specs=[pl.BlockSpec(memory_space=pl.ANY), vmem, vmem],
        out_specs=(pl.BlockSpec(memory_space=pl.ANY), vmem),
        scratch_shapes=[
            pltpu.VMEM((row_count, col_count), BF16),
            dma,
            pltpu.VMEM((owned, col_count), F32),
            dma,
            pltpu.VMEM((row_count // LANES, LANES), F32),
            pltpu.VMEM((col_count, col_count), F32),
            pltpu.VMEM((4, 2, owned, half), F32),
            pltpu.VMEM((4, 2, owned, half), F32),
            pltpu.VMEM((4, 2, owned, half), F32),
            pltpu.VMEM((2, 3, owned, half), F32),
            dma((4,)), dma((4,)),
            dma((2, 3)), dma((2, 3)),
        ]
        + chunk_scratch(quarter * 3 // 2, quarter)
        + chunk_scratch(quarter * 7 // 2, quarter),
        compiler_params=pltpu.CompilerParams(
            collective_id=0, has_side_effects=True, vmem_limit_bytes=60 * 1024 * 1024
        ),
        name="embed",
    )(design, scales.reshape(-1, LANES), buckets.reshape(-1, LANES))


def solution(mesh):
    in_specs = (P(("grp", "row"), None), P(("grp", "row")), P(("grp", "row")))
    out_specs = (P(("grp", "row"), None), P("grp", None))
    fast = mesh.shape["grp"] == 4 and mesh.shape["row"] == 8
    return jax.shard_map(
        per_device_fast if fast else per_device_general,
        mesh=mesh, in_specs=in_specs, out_specs=out_specs, check_vma=False,
    )
```

time: 289 us -> 72.1 us (0.25)
  waiting for transfers between devices: 129 us -> 0 us
  other arithmetic: 83.4 us -> 0 us
  Pallas kernels: 0 us -> 67.8 us
  blocking collectives: 42.9 us -> 0 us
  between operations: 16.7 us -> 0.64 us
  matrix products: 10.9 us -> 0 us
    psum x1 -> x0, waiting for transfers between devices: 129 us -> none  [per_device(): whole_gram = lax.psum(local_gram, ('grp', 'row'))]
    another operation x14 -> x0, other arithmetic: 78.6 us -> none  [chol_upper(): return jnp.linalg.cholesky(gram_matrix).T]
    pallas_call x0 -> x1, Pallas kernels: none -> 67.8 us  [per_device_fast(): pl.pallas_call(functools.partial(embed_kernel, 1.0 / math.sqrt(row_count...]
    all_to_all x1 -> x0, blocking collectives: 42.9 us -> none  [per_device(): lax.all_to_all(partial_value, 'row', split_axis=0, concat_axis=0, tiled=T...]
    another operation x6 -> x0, matrix products: 5.46 us -> none  [chol_upper(): return jnp.linalg.cholesky(gram_matrix).T]
    dot_general x2 -> x0, matrix products: 5.45 us -> none  [the longest x1 3.31 us: per_device(): jnp.dot(onehot_table, design, preferred_element_type=jnp.float32)]
  transfers between devices with their start and end apart: 1 -> 0, of which waited for: 1 -> 0; matrix products, arithmetic and copies ran while one was open for 0% -> 0% of each run, Pallas kernels for 0% -> 0%
where the time goes in v3:
time: 72.1 us; the launch traced here: 71.9 us
  Pallas kernels  67.8 us (94%)
  local copies, waits for them, and re-layouts  3.44 us (5%)
    pallas_call x1, Pallas kernels, per_device_fast(): pl.pallas_call(functools.partial(embed_kernel, 1.0 / math.sqrt(row_count...  67.8 us
    unnamed x2, local copies, waits for them, and re-layouts  3.44 us

profile of v3, /device:TPU:0, one launch (start us, length us, event | category | flops | bytes accessed | tf_op | source)
XLA Modules:
  0.0 71.9 jit_solution(5888102569698403703)
XLA Ops:
  0.6 67.8 %embed.1 = (f32[192,512]{1,0:T(8,128)}, f32[128,512]{1,0:T(8,128)}) custom-call(bf16[1536,512]{1,0:T(8,128)(2,1)} %design_hbm.1, bf16[12,128]{1,0:T(8,128)(2,1)} %bitcast.3, s32[12,128]{1,0:T(8,128)} %bitcast.2), custom_call_target="tpu_custom_call" | custom-call | tf_op jit(solution)/shard_map/embed/pallas_call | solution.py:473
  68.4 1.8 %copy.7 = f32[192,512]{1,0:T(8,128)} copy(f32[192,512]{1,0:T(8,128)} %get-tuple-element.4) | data formatting | bytes 786432
  70.2 1.7 %copy.8 = f32[128,512]{1,0:T(8,128)} copy(f32[128,512]{1,0:T(8,128)} %get-tuple-element.5) | data formatting | bytes 524288

commit v4 on v3

v4 whole, which is shorter than its diff:
```python
import functools
import math

import jax
import jax.numpy as jnp
from jax import lax
from jax.experimental import pallas as pl
from jax.experimental.pallas import tpu as pltpu
from jax.sharding import PartitionSpec as P

MESH = pl.DeviceIdType.MESH
F32 = jnp.float32
BF16 = jnp.bfloat16
LANES = 128
PANEL = 16


def split3(value):
    high = value.astype(BF16)
    rest = value - high.astype(F32)
    mid = rest.astype(BF16)
    low = (rest - mid.astype(F32)).astype(BF16)
    return high, mid, low


def panel_factor(panel, offset):
    size, width = panel.shape
    tiles = width // LANES
    sub = lax.broadcasted_iota(jnp.int32, (size, LANES), 0)
    cols = [
        jnp.broadcast_to(panel[:, offset + k : offset + k + 1], (size, LANES))
        for k in range(size)
    ]
    parts = [panel[:, t * LANES : (t + 1) * LANES] for t in range(tiles)]
    scale = jnp.zeros((size, LANES), F32)
    for j in range(size):
        inv = lax.rsqrt(cols[j][j : j + 1, :])
        mult = cols[j] * inv
        scale = jnp.where(sub == j, inv, scale)
        for k in range(j + 1, size):
            cols[k] = cols[k] - mult * (cols[k][j : j + 1, :] * inv)
        below = jnp.where(sub > j, mult, 0.0)
        parts = [part - below * (part[j : j + 1, :] * inv) for part in parts]
    return [part * scale for part in parts]


def factor_block(work, base, stop, hook=None):
    for start in range(0, LANES, PANEL):
        row = base + start
        rows = panel_factor(work[row : row + PANEL, base:stop], start)
        for t, part in enumerate(rows):
            work[row : row + PANEL, base + t * LANES : base + (t + 1) * LANES] = part
        if hook is not None:
            hook()
        if start + PANEL == LANES:
            break
        splits = [split3(part) for part in rows]
        h, m, l = splits[0]
        lhs = jnp.concatenate([h, h, m, h, l, m], axis=0)
        for t, (h, m, l) in enumerate(splits):
            rhs = jnp.concatenate([h, m, h, l, h, m], axis=0)
            prod = lax.dot_general(lhs, rhs, (((0,), (0,)), ((), ())), preferred_element_type=F32)
            cs = slice(base + t * LANES, base + (t + 1) * LANES)
            work[row + PANEL : base + LANES, cs] = (
                work[row + PANEL : base + LANES, cs] - prod[start + PANEL :, :]
            )


def tdot(left, right):
    return lax.dot_general(
        left, right, (((0,), (0,)), ((), ())),
        precision=lax.Precision.HIGHEST, preferred_element_type=F32,
    )


def trail(work, base, last, stop):
    for left in range(base + LANES, last, LANES):
        work[left : left + LANES, left:stop] = work[left : left + LANES, left:stop] - tdot(
            work[base : base + LANES, left : left + LANES], work[base : base + LANES, left:stop]
        )


def write_rows(grp, scale, out_ref, work):
    size = work.shape[0]
    count = out_ref.shape[0]
    first = pl.multiple_of(grp * count, count)
    rows = first + lax.broadcasted_iota(jnp.int32, (count, size), 0)
    cols = lax.broadcasted_iota(jnp.int32, (count, size), 1)
    value = work[pl.ds(first, count), :] * scale
    out_ref[...] = jnp.where(cols >= rows, value, 0.0)


def factor_kernel(scale, gram_ref, out_ref, work):
    size = work.shape[0]
    work[...] = gram_ref[...]
    for base in range(0, size, LANES):
        factor_block(work, base, size)
        trail(work, base, size, size)
    write_rows(lax.axis_index("grp"), scale, out_ref, work)


def factor_packed_kernel(scale, gram_ref, sketch_ref, out_ref, sketch_out, work, copy_sem):
    copy = pltpu.make_async_copy(sketch_ref, sketch_out, copy_sem)
    copy.start()
    size = work.shape[0]
    half = size // 2
    q = half // 2
    work[0:q] = gram_ref[0:q]
    work[q:half, q:] = gram_ref[q:half, q:]
    work[3 * q :, 3 * q :] = gram_ref[q:half, 0:q]
    work[half : half + q // 2, half:] = gram_ref[half:, 0:half]
    work[half + q // 2 : 3 * q, half:] = gram_ref[half:, half:]
    for base in range(0, size, LANES):
        factor_block(work, base, size)
        trail(work, base, size, size)
    write_rows(lax.axis_index("grp"), scale, out_ref, work)
    copy.wait()


def factor_call(gram, slab_rows, scale):
    size = gram.shape[0]
    vmem = pl.BlockSpec(memory_space=pltpu.VMEM)
    return pl.pallas_call(
        functools.partial(factor_kernel, scale),
        out_shape=jax.ShapeDtypeStruct((slab_rows, size), F32),
        in_specs=[vmem],
        out_specs=vmem,
        scratch_shapes=[pltpu.VMEM((size, size), F32)],
        compiler_params=pltpu.CompilerParams(vmem_limit_bytes=32 * 1024 * 1024),
        name="factor",
    )(gram)


def self_gram(matrix):
    return lax.dot_general(
        matrix,
        matrix,
        (((0,), (0,)), ((), ())),
        precision=lax.Precision.HIGHEST,
        preferred_element_type=F32,
    )


def per_device_general(design, scales, buckets):
    row_count = design.shape[0]
    col_count = design.shape[1]
    row_parts = lax.axis_size("row")
    owned_rows = row_count // row_parts
    label_ids = lax.iota(jnp.int32, row_count)
    onehot_table = jnp.where(
        label_ids[:, None] == buckets[None, :], scales[None, :], jnp.zeros((), BF16)
    )
    partial_value = jnp.dot(onehot_table, design, preferred_element_type=F32).reshape(
        row_parts, owned_rows, col_count
    )
    arrived = lax.all_to_all(partial_value, "row", split_axis=0, concat_axis=0, tiled=True)
    sketch = jnp.sum(arrived, axis=0)
    whole_gram = lax.psum(self_gram(sketch), ("grp", "row"))
    grp_count = lax.axis_size("grp")
    scale = 1.0 / math.sqrt(row_count * grp_count)
    slab = factor_call(whole_gram, col_count // grp_count, scale)
    return (sketch, slab)


def embed_kernel(
    design_ref, scales_in, buckets_ref, sketch_ref, gram_ref, scales_ref,
    give, took, acc, near, gsum, gcore, gown, gnear, gz, gquart, gall,
    give_s, give_r, near_s, near_r, gcore_s, gcore_r, gnear_s, gnear_r, gz_s, gz_r,
    gback_s, gback_r, gpair_s, gpair_r,
):
    z = lax.axis_index("grp")
    row = lax.axis_index("row")
    c = lax.rem(row, 2)
    x = lax.rem(row // 2, 2)
    y = row // 4
    core_id = (z, row + 1 - 2 * c)
    x_id = (z, row + 2 - 4 * x)
    y_id = (z, row + 4 - 8 * y)
    diag_id = (z, 7 - row + 2 * c - 1)
    peers = [core_id, x_id, y_id, diag_id] + [(lax.rem(z + d, 4), row) for d in (1, 2, 3)]

    barrier = pltpu.get_barrier_semaphore()
    for peer in peers:
        pl.semaphore_signal(barrier, inc=1, device_id=peer, device_id_type=MESH)

    pending = []

    def send(src, dst, send_sem, recv_sem, peer):
        copy = pltpu.make_async_remote_copy(
            src_ref=src, dst_ref=dst, send_sem=send_sem, recv_sem=recv_sem,
            device_id=peer, device_id_type=MESH,
        )
        copy.start()
        pending.append(copy)
        return copy

    scales_ref[...] = scales_in[...].astype(F32)
    rows_all = design_ref.shape[0]
    owned = sketch_ref.shape[0]
    half = design_ref.shape[1] // 2

    def part(slot):
        ty = y if slot < 2 else 1 - y
        tx = x if slot % 2 == 0 else 1 - x
        base = (ty * 4 + tx * 2) * owned
        ids = lax.broadcasted_iota(jnp.int32, (owned, LANES), 0) + base
        labels = jnp.concatenate([ids + (1 - c) * owned, ids + c * owned], axis=0)
        table = jnp.concatenate(
            [
                jnp.where(labels == buckets_ref[k : k + 1, :], scales_ref[k : k + 1, :], 0.0).astype(BF16)
                for k in range(rows_all // LANES)
            ],
            axis=1,
        )
        value = jnp.dot(table, design_ref[...], preferred_element_type=F32)
        for h in range(2):
            give[slot, h] = value[:owned, h * half : (h + 1) * half]
            acc[slot, h] = value[owned:, h * half : (h + 1) * half]

    first = (x_id, y_id)
    second = (y_id, x_id)
    passed = (2, 1)
    direct = (1, 2)

    def near_send(slot, h, step):
        peer = second[h] if step == 2 else first[h]
        return send(acc.at[slot, h], near.at[h, step], near_s.at[h, step], near_r.at[h, step], peer)

    steps = {}
    from_core = {}
    order = (3, 2, 1, 0)

    def give_core(slot):
        from_core[slot] = send(give.at[slot], took.at[slot], give_s.at[slot], give_r.at[slot], core_id)

    def take_core(slot):
        from_core[slot].wait_recv()
        for h in range(2):
            acc[slot, h] = acc[slot, h] + took[slot, h]
            if slot == 3:
                steps[h, 0] = near_send(slot, h, 0)
            elif slot == direct[h]:
                steps[h, 1] = near_send(slot, h, 1)

    part(3)
    pl.semaphore_wait(barrier, len(peers))
    give_core(3)
    part(2)
    give_core(2)
    take_core(3)
    part(1)
    give_core(1)
    take_core(2)
    part(0)
    give_core(0)
    take_core(1)
    take_core(0)
    for h in range(2):
        steps[h, 0].wait_recv()
        acc[passed[h], h] = acc[passed[h], h] + near[h, 0]
        steps[h, 2] = near_send(passed[h], h, 2)
    for h in range(2):
        steps[h, 1].wait_recv()
        acc[0, h] = acc[0, h] + near[h, 1]
    for h in range(2):
        steps[h, 2].wait_recv()
        sketch_ref[:, h * half : (h + 1) * half] = acc[0, h] + near[h, 2]

    q = half // 2

    def cut(i, j):
        return sketch_ref[:, i * q : j * q]

    gsum[0:q] = tdot(cut(0, 1), cut(0, 4))
    gsum[q:half, q:] = tdot(cut(1, 2), cut(1, 4))
    gsum[q:half, 0:q] = tdot(cut(3, 4), cut(3, 4))
    value = tdot(cut(2, 3), cut(2, 4))
    gsum[half:, 0:half] = value[: q // 2]
    gsum[half:, half:] = value[q // 2 :]

    packed = gsum.shape[0]
    core_rows = packed // 2
    piece = packed // 8
    theirs = pl.ds(pl.multiple_of((1 - c) * core_rows, 8), core_rows)
    ours = pl.ds(pl.multiple_of(c * core_rows, 8), core_rows)
    send(gsum.at[theirs], gcore, gcore_s, gcore_r, core_id).wait_recv()

    def chip(slot):
        cy = y if slot < 2 else 1 - y
        cx = x if slot % 2 == 0 else 1 - x
        return pl.multiple_of((cy * 2 + cx) * piece, 8)

    plane_ids = {1: x_id, 2: y_id, 3: diag_id}
    gown[...] = gsum[ours] + gcore[...]
    copies = {
        slot: send(
            gown.at[pl.ds(chip(slot), piece)], gnear.at[slot - 1],
            gnear_s.at[slot - 1], gnear_r.at[slot - 1], plane_ids[slot],
        )
        for slot in (3, 1, 2)
    }
    total = gown[pl.ds(chip(0), piece)]
    for slot in (1, 2, 3):
        copies[slot].wait_recv()
        total = total + gnear[slot - 1]
    gz[0] = total

    def lanes_of(place):
        return pl.ds(pl.multiple_of(place * q, q), q)

    z_places = [lax.rem(z + d, 4) for d in (1, 2, 3)]
    copies = [
        send(
            gz.at[0, :, lanes_of(place)], gquart.at[d], gz_s.at[d], gz_r.at[d], (place, row)
        )
        for d, place in enumerate(z_places)
    ]
    mine = lanes_of(z)
    total = gz[0, :, mine]
    for d in range(3):
        copies[d].wait_recv()
        total = total + gquart[d]
    at = pl.ds(pl.multiple_of(c * core_rows + chip(0), 8), piece)
    gall[at, mine] = total
    for d, place in enumerate(z_places):
        ref = gall.at[at, mine]
        send(ref, ref, gz_s.at[3 + d], gz_r.at[3 + d], (place, row))
    for d in range(3):
        ref = gall.at[at, lanes_of(lax.rem(z + 3 - d, 4))]
        pltpu.make_async_remote_copy(
            src_ref=ref, dst_ref=ref, send_sem=gz_s.at[3 + d], recv_sem=gz_r.at[3 + d],
            device_id=core_id, device_id_type=MESH,
        ).wait_recv()

    def place(slot, core):
        return gall.at[pl.ds(pl.multiple_of(core * core_rows + chip(slot), 8), piece)]

    def landed(ref, sems, step):
        pltpu.make_async_remote_copy(
            src_ref=ref, dst_ref=ref, send_sem=gcore_s, recv_sem=sems.at[step],
            device_id=core_id, device_id_type=MESH,
        ).wait_recv()

    for slot in (3, 1, 2):
        send(place(0, c), place(0, c), gback_s.at[slot], gback_r.at[slot], plane_ids[slot])
    send(place(0, c), place(0, c), gpair_s.at[0], gpair_r.at[0], core_id)
    for slot in (1, 2, 3):
        landed(place(slot, c), gback_r, slot)
        send(place(slot, c), place(slot, c), gpair_s.at[slot], gpair_r.at[slot], core_id)
    for slot in range(4):
        landed(place(slot, 1 - c), gpair_r, slot)

    gram_ref[...] = gall[...]
    for copy in pending:
        copy.wait_send()


def per_device_fast(design, scales, buckets):
    row_count, col_count = design.shape
    owned = row_count // lax.axis_size("row")
    half = col_count // 2
    quarter = half // 2
    packed = quarter * 5 // 2
    grp_count = lax.axis_size("grp")
    dma = pltpu.SemaphoreType.DMA
    vmem = pl.BlockSpec(memory_space=pltpu.VMEM)
    sketch, gram = pl.pallas_call(
        embed_kernel,
        out_shape=(
            jax.ShapeDtypeStruct((owned, col_count), F32),
            jax.ShapeDtypeStruct((packed, col_count), F32),
        ),
        in_specs=[vmem, vmem, vmem],
        out_specs=(vmem, vmem),
        scratch_shapes=[
            pltpu.VMEM((row_count // LANES, LANES), F32),
            pltpu.VMEM((4, 2, owned, half), F32),
            pltpu.VMEM((4, 2, owned, half), F32),
            pltpu.VMEM((4, 2, owned, half), F32),
            pltpu.VMEM((2, 3, owned, half), F32),
            pltpu.VMEM((packed, col_count), F32),
            pltpu.VMEM((packed // 2, col_count), F32),
            pltpu.VMEM((packed // 2, col_count), F32),
            pltpu.VMEM((3, packed // 8, col_count), F32),
            pltpu.VMEM((1, packed // 8, col_count), F32),
            pltpu.VMEM((3, packed // 8, quarter), F32),
            pltpu.VMEM((packed, col_count), F32),
            dma((4,)), dma((4,)),
            dma((2, 3)), dma((2, 3)),
            dma, dma,
            dma((3,)), dma((3,)),
            dma((6,)), dma((6,)),
            dma((4,)), dma((4,)),
            dma((4,)), dma((4,)),
        ],
        compiler_params=pltpu.CompilerParams(
            collective_id=0, has_side_effects=True, vmem_limit_bytes=40 * 1024 * 1024
        ),
        name="embed",
    )(design, scales.reshape(-1, LANES), buckets.reshape(-1, LANES))
    slab, sketch = pl.pallas_call(
        functools.partial(factor_packed_kernel, 1.0 / math.sqrt(row_count * grp_count)),
        out_shape=(
            jax.ShapeDtypeStruct((col_count // grp_count, col_count), F32),
            jax.ShapeDtypeStruct((owned, col_count), F32),
        ),
        in_specs=[vmem, pl.BlockSpec(memory_space=pl.ANY)],
        out_specs=(vmem, pl.BlockSpec(memory_space=pl.ANY)),
        scratch_shapes=[pltpu.VMEM((col_count, col_count), F32), dma],
        compiler_params=pltpu.CompilerParams(vmem_limit_bytes=32 * 1024 * 1024),
        name="factor",
    )(gram, sketch)
    return (sketch, slab)


def solution(mesh):
    in_specs = (P(("grp", "row"), None), P(("grp", "row")), P(("grp", "row")))
    out_specs = (P(("grp", "row"), None), P("grp", None))
    fast = mesh.shape["grp"] == 4 and mesh.shape["row"] == 8
    return jax.shard_map(
        per_device_fast if fast else per_device_general,
        mesh=mesh, in_specs=in_specs, out_specs=out_specs, check_vma=False,
    )
```

time: 72.1 us -> 61.5 us (0.85)
  Pallas kernels: 67.8 us -> 57.8 us
    pallas_call x1 -> x2, Pallas kernels: 67.8 us -> 57.8 us  [the longest x1 43 us: per_device_fast(): pl.pallas_call(embed_kernel, out_shape=(jax.ShapeDtypeStruct((owned, col_...]
    unnamed x2 -> x6, local copies, waits for them, and re-layouts: 3.44 us -> 2.78 us
where the time goes in v4:
time: 61.5 us; the launch traced here: 61.2 us
  Pallas kernels  57.8 us (94%)
  local copies, waits for them, and re-layouts  2.78 us (5%)
  between operations  0.65 us (1%)
    pallas_call x1, Pallas kernels, per_device_fast(): pl.pallas_call(embed_kernel, out_shape=(jax.ShapeDtypeStruct((owned, col_...  43 us
    pallas_call x1, Pallas kernels, per_device_fast(): pl.pallas_call(functools.partial(factor_packed_kernel, 1.0 / math.sqrt(ro...  14.8 us
    unnamed x6, local copies, waits for them, and re-layouts  2.78 us

profile of v4, /device:TPU:0, one launch (start us, length us, event | category | flops | bytes accessed | tf_op | source)
XLA Modules:
  0.0 61.2 jit_solution(435410710147356233)
XLA Ops:
  0.6 0.0 copy-start
  0.6 1.4 %copy-done = bf16[1536,512]{1,0:T(8,128)(2,1)S(1)} copy-done((bf16[1536,512]{1,0:T(8,128)(2,1)S(1)}, bf16[1536,512]{1,0:T(8,128)(2,1)}, u32[]{:S(2)}) %copy-start) | copy-done | bytes 1572888
  2.0 0.0 copy-start.1
  2.0 0.7 %copy-done.1 = s32[1536]{0:T(1024)S(1)} copy-done((s32[1536]{0:T(1024)S(1)}, s32[1536]{0:T(1024)}, u32[]{:S(2)}) %copy-start.1) | copy-done | bytes 6168
  2.7 0.0 copy-start.2
  2.7 0.7 %copy-done.2 = bf16[1536]{0:T(1024)(128)(2,1)S(1)} copy-done((bf16[1536]{0:T(1024)(128)(2,1)S(1)}, bf16[1536]{0:T(1024)(128)(2,1)}, u32[]{:S(2)}) %copy-start.2) | copy-done | bytes 3096
  3.4 43.0 %embed.1 = (f32[192,512]{1,0:T(8,128)S(1)}, f32[320,512]{1,0:T(8,128)S(1)}) custom-call(bf16[1536,512]{1,0:T(8,128)(2,1)S(1)} %copy-done, bf16[12,128]{1,0:T(8,128)(2,1)S(1)} %bitcast.3, s32[12,128]{1,0:T(8,128)S(1)} %bitcast.2), custom_call_target="tpu_custom_call" | custom-call | tf_op jit(solution)/shard_map/embed/pallas_call | solution.py:367
  46.4 14.8 %factor.1 = (f32[128,512]{1,0:T(8,128)}, f32[192,512]{1,0:T(8,128)}) custom-call(f32[320,512]{1,0:T(8,128)S(1)} %get-tuple-element.6.gram_ref, f32[192,512]{1,0:T(8,128)S(1)} %get-tuple-element.7.sketch_ref), custom_call_target="tpu_custom_call" | custom-call | tf_op jit(solution)/shard_map/factor/pallas_call | solution.py:401
Async XLA Ops:
  0.6 1.4 %copy-start = (bf16[1536,512]{1,0:T(8,128)(2,1)S(1)}, bf16[1536,512]{1,0:T(8,128)(2,1)}, u32[]{:S(2)}) copy-start(bf16[1536,512]{1,0:T(8,128)(2,1)} %design_ref.1) | copy-start | bytes 4718596
  2.0 0.7 %copy-start.1 = (s32[1536]{0:T(1024)S(1)}, s32[1536]{0:T(1024)}, u32[]{:S(2)}) copy-start(s32[1536]{0:T(1024)} %param.5) | copy-start | bytes 18436
  2.7 0.7 %copy-start.2 = (bf16[1536]{0:T(1024)(128)(2,1)S(1)}, bf16[1536]{0:T(1024)(128)(2,1)}, u32[]{:S(2)}) copy-start(bf16[1536]{0:T(1024)(128)(2,1)} %param.4) | copy-start | bytes 9220

commit v5 on v4

--- a/solution.py
+++ b/solution.py
@@ -26,22 +26,41 @@
 def panel_factor(panel, offset):
     size, width = panel.shape
     tiles = width // LANES
-    sub = lax.broadcasted_iota(jnp.int32, (size, LANES), 0)
-    cols = [
-        jnp.broadcast_to(panel[:, offset + k : offset + k + 1], (size, LANES))
+    bands = size // 8
+    sub = lax.broadcasted_iota(jnp.int32, (8, LANES), 0)
+    cols = {
+        (b, k): jnp.broadcast_to(
+            panel[8 * b : 8 * b + 8, offset + k : offset + k + 1], (8, LANES)
+        )
         for k in range(size)
+        for b in range(k // 8, bands)
+    }
+    parts = {
+        (b, t): panel[8 * b : 8 * b + 8, t * LANES : (t + 1) * LANES]
+        for b in range(bands)
+        for t in range(tiles)
+    }
+    scale = [jnp.zeros((8, LANES), F32) for _ in range(bands)]
+    for j in range(size):
+        jb, jr = j // 8, j % 8
+        inv = lax.rsqrt(cols[jb, j][jr : jr + 1, :])
+        mult = {b: cols[b, j] * inv for b in range(jb, bands)}
+        scale[jb] = jnp.where(sub == jr, inv, scale[jb])
+        for k in range(j + 1, size):
+            other = mult[k // 8][k % 8 : k % 8 + 1, :]
+            for b in range(k // 8, bands):
+                cols[b, k] = cols[b, k] - mult[b] * other
+        pivots = [parts[jb, t][jr : jr + 1, :] * inv for t in range(tiles)]
+        for b in range(jb, bands):
+            if b == jb and jr == 7:
+                continue
+            below = jnp.where(sub > jr, mult[b], 0.0) if b == jb else mult[b]
+            for t in range(tiles):
+                parts[b, t] = parts[b, t] - below * pivots[t]
+    return [
+        jnp.concatenate([parts[b, t] * scale[b] for b in range(bands)], axis=0)
+        for t in range(tiles)
     ]
-    parts = [panel[:, t * LANES : (t + 1) * LANES] for t in range(tiles)]
-    scale = jnp.zeros((size, LANES), F32)
-    for j in range(size):
-        inv = lax.rsqrt(cols[j][j : j + 1, :])
-        mult = cols[j] * inv
-        scale = jnp.where(sub == j, inv, scale)
-        for k in range(j + 1, size):
-            cols[k] = cols[k] - mult * (cols[k][j : j + 1, :] * inv)
-        below = jnp.where(sub > j, mult, 0.0)
-        parts = [part - below * (part[j : j + 1, :] * inv) for part in parts]
-    return [part * scale for part in parts]
 
 
 def factor_block(work, base, stop, hook=None):
@@ -163,7 +182,8 @@
 
 
 def embed_kernel(
-    design_ref, scales_in, buckets_ref, sketch_ref, gram_ref, scales_ref,
+    design_hbm, scales_in, buckets_ref, sketch_ref, gram_ref,
+    design_ref, load_s, scales_ref,
     give, took, acc, near, gsum, gcore, gown, gnear, gz, gquart, gall,
     give_s, give_r, near_s, near_r, gcore_s, gcore_r, gnear_s, gnear_r, gz_s, gz_r,
     gback_s, gback_r, gpair_s, gpair_r,
@@ -179,6 +199,8 @@
     diag_id = (z, 7 - row + 2 * c - 1)
     peers = [core_id, x_id, y_id, diag_id] + [(lax.rem(z + d, 4), row) for d in (1, 2, 3)]
 
+    load = pltpu.make_async_copy(design_hbm, design_ref, load_s)
+    load.start()
     barrier = pltpu.get_barrier_semaphore()
     for peer in peers:
         pl.semaphore_signal(barrier, inc=1, device_id=peer, device_id_type=MESH)
@@ -212,6 +234,8 @@
             ],
             axis=1,
         )
+        if slot == 3:
+            load.wait()
         value = jnp.dot(table, design_ref[...], preferred_element_type=F32)
         for h in range(2):
             give[slot, h] = value[:owned, h * half : (h + 1) * half]
@@ -370,9 +394,11 @@
             jax.ShapeDtypeStruct((owned, col_count), F32),
             jax.ShapeDtypeStruct((packed, col_count), F32),
         ),
-        in_specs=[vmem, vmem, vmem],
+        in_specs=[pl.BlockSpec(memory_space=pl.ANY), vmem, vmem],
         out_specs=(vmem, vmem),
         scratch_shapes=[
+            pltpu.VMEM((row_count, col_count), BF16),
+            dma,
             pltpu.VMEM((row_count // LANES, LANES), F32),
             pltpu.VMEM((4, 2, owned, half), F32),
             pltpu.VMEM((4, 2, owned, half), F32),
@@ -394,7 +420,7 @@
             dma((4,)), dma((4,)),
         ],
         compiler_params=pltpu.CompilerParams(
-            collective_id=0, has_side_effects=True, vmem_limit_bytes=40 * 1024 * 1024
+            collective_id=0, has_side_effects=True, vmem_limit_bytes=52 * 1024 * 1024
         ),
         name="embed",
     )(design, scales.reshape(-1, LANES), buckets.reshape(-1, LANES))

time: 61.5 us -> 59.9 us (0.974)
  local copies, waits for them, and re-layouts: 2.78 us -> 1.38 us
    unnamed x6 -> x4, local copies, waits for them, and re-layouts: 2.78 us -> 1.38 us
where the time goes in v5:
time: 59.9 us; the launch traced here: 59.7 us
  Pallas kernels  57.6 us (96%)
  local copies, waits for them, and re-layouts  1.38 us (2%)
  between operations  0.65 us (1%)
    pallas_call x1, Pallas kernels, per_device_fast(): pl.pallas_call(embed_kernel, out_shape=(jax.ShapeDtypeStruct((owned, col_...  43 us
    pallas_call x1, Pallas kernels, per_device_fast(): pl.pallas_call(functools.partial(factor_packed_kernel, 1.0 / math.sqrt(ro...  14.6 us
    unnamed x4, local copies, waits for them, and re-layouts  1.38 us

profile of v5, /device:TPU:0, one launch (start us, length us, event | category | flops | bytes accessed | tf_op | source)
XLA Modules:
  0.0 59.7 jit_solution(13615106563307889046)
XLA Ops:
  0.6 0.0 copy-start
  0.6 0.7 %copy-done = s32[1536]{0:T(1024)S(1)} copy-done((s32[1536]{0:T(1024)S(1)}, s32[1536]{0:T(1024)}, u32[]{:S(2)}) %copy-start) | copy-done | bytes 6168
  1.3 0.0 copy-start.1
  1.3 0.7 %copy-done.1 = bf16[1536]{0:T(1024)(128)(2,1)S(1)} copy-done((bf16[1536]{0:T(1024)(128)(2,1)S(1)}, bf16[1536]{0:T(1024)(128)(2,1)}, u32[]{:S(2)}) %copy-start.1) | copy-done | bytes 3096
  2.0 43.0 %embed.1 = (f32[192,512]{1,0:T(8,128)S(1)}, f32[320,512]{1,0:T(8,128)S(1)}) custom-call(bf16[1536,512]{1,0:T(8,128)(2,1)} %design_hbm.1, bf16[12,128]{1,0:T(8,128)(2,1)S(1)} %bitcast.3, s32[12,128]{1,0:T(8,128)S(1)} %bitcast.2), custom_call_target="tpu_custom_call" | custom-call | tf_op jit(solution)/shard_map/embed/pallas_call | solution.py:391
  45.0 14.6 %factor.1 = (f32[128,512]{1,0:T(8,128)}, f32[192,512]{1,0:T(8,128)}) custom-call(f32[320,512]{1,0:T(8,128)S(1)} %get-tuple-element.6.gram_ref, f32[192,512]{1,0:T(8,128)S(1)} %get-tuple-element.7.sketch_ref), custom_call_target="tpu_custom_call" | custom-call | tf_op jit(solution)/shard_map/factor/pallas_call | solution.py:427
Async XLA Ops:
  0.6 0.7 %copy-start = (s32[1536]{0:T(1024)S(1)}, s32[1536]{0:T(1024)}, u32[]{:S(2)}) copy-start(s32[1536]{0:T(1024)} %param.5) | copy-start | bytes 18436
  1.3 0.7 %copy-start.1 = (bf16[1536]{0:T(1024)(128)(2,1)S(1)}, bf16[1536]{0:T(1024)(128)(2,1)}, u32[]{:S(2)}) copy-start(bf16[1536]{0:T(1024)(128)(2,1)} %param.4) | copy-start | bytes 9220

commit v6 on v5

--- a/solution.py
+++ b/solution.py
@@ -12,7 +12,7 @@
 F32 = jnp.float32
 BF16 = jnp.bfloat16
 LANES = 128
-PANEL = 16
+PANEL = 32
 
 
 def split3(value):

time: 59.9 us -> 58.8 us (0.982)
  Pallas kernels: 57.6 us -> 56.6 us
    pallas_call x1, Pallas kernels: 14.6 us -> 13.5 us  [per_device_fast(): pl.pallas_call(functools.partial(factor_packed_kernel, 1.0 / math.sqrt(ro...]
where the time goes in v6:
time: 58.8 us; the launch traced here: 58.6 us
  Pallas kernels  56.6 us (96%)
  local copies, waits for them, and re-layouts  1.38 us (2%)
  between operations  0.65 us (1%)
    pallas_call x1, Pallas kernels, per_device_fast(): pl.pallas_call(embed_kernel, out_shape=(jax.ShapeDtypeStruct((owned, col_...  43 us
    pallas_call x1, Pallas kernels, per_device_fast(): pl.pallas_call(functools.partial(factor_packed_kernel, 1.0 / math.sqrt(ro...  13.5 us
    unnamed x4, local copies, waits for them, and re-layouts  1.38 us

profile of v6, /device:TPU:0, one launch (start us, length us, event | category | flops | bytes accessed | tf_op | source)
XLA Modules:
  0.0 58.6 jit_solution(13680764284033377492)
XLA Ops:
  0.6 0.0 copy-start
  0.6 0.7 %copy-done = s32[1536]{0:T(1024)S(1)} copy-done((s32[1536]{0:T(1024)S(1)}, s32[1536]{0:T(1024)}, u32[]{:S(2)}) %copy-start) | copy-done | bytes 6168
  1.3 0.0 copy-start.1
  1.3 0.7 %copy-done.1 = bf16[1536]{0:T(1024)(128)(2,1)S(1)} copy-done((bf16[1536]{0:T(1024)(128)(2,1)S(1)}, bf16[1536]{0:T(1024)(128)(2,1)}, u32[]{:S(2)}) %copy-start.1) | copy-done | bytes 3096
  2.0 43.0 %embed.1 = (f32[192,512]{1,0:T(8,128)S(1)}, f32[320,512]{1,0:T(8,128)S(1)}) custom-call(bf16[1536,512]{1,0:T(8,128)(2,1)} %design_hbm.1, bf16[12,128]{1,0:T(8,128)(2,1)S(1)} %bitcast.3, s32[12,128]{1,0:T(8,128)S(1)} %bitcast.2), custom_call_target="tpu_custom_call" | custom-call | tf_op jit(solution)/shard_map/embed/pallas_call | solution.py:391
  45.0 13.5 %factor.1 = (f32[128,512]{1,0:T(8,128)}, f32[192,512]{1,0:T(8,128)}) custom-call(f32[320,512]{1,0:T(8,128)S(1)} %get-tuple-element.6.gram_ref, f32[192,512]{1,0:T(8,128)S(1)} %get-tuple-element.7.sketch_ref), custom_call_target="tpu_custom_call" | custom-call | tf_op jit(solution)/shard_map/factor/pallas_call | solution.py:427
Async XLA Ops:
  0.6 0.7 %copy-start = (s32[1536]{0:T(1024)S(1)}, s32[1536]{0:T(1024)}, u32[]{:S(2)}) copy-start(s32[1536]{0:T(1024)} %param.5) | copy-start | bytes 18436
  1.3 0.7 %copy-start.1 = (bf16[1536]{0:T(1024)(128)(2,1)S(1)}, bf16[1536]{0:T(1024)(128)(2,1)}, u32[]{:S(2)}) copy-start(bf16[1536]{0:T(1024)(128)(2,1)} %param.4) | copy-start | bytes 9220
